TPU v7x, 32 devices: a whole 2x2x4 slice. The times are simulated.
32 devices in a mesh: seq: 8 (over y, x, core), tp: 4 (over z).
Axes of the slice: x: 2, y: 2, z: 4, core: 2. Of those that a mesh axis runs over, the one named last changes fastest.
Arguments:
- hidden: bfloat16 [2048, 1024], P('seq'), may hold values from -6 to 6
- segment_ids: int32 [2048], replicated, may hold values from 0 to 3, never falling along the last dimension, each value on 1 to 1536 neighbouring positions
- routes: int32 [2048, 8], P('seq'), may hold values from 0 to 31, all different within a row; in each aligned block of 256 rows (0 to 255, 256 to 511, ...) at most 128 rows name the same one
- gates: float32 [2048, 8], P('seq'), may hold values from 0.02 to 0.25
- norm_attn: bfloat16 [1024], replicated, may hold values from 0.5 to 1.5
- norm_moe: bfloat16 [1024], replicated, may hold values from 0.5 to 1.5
- w_query: bfloat16 [1024, 1024], P(None, 'tp')
- w_key: bfloat16 [1024, 512], P(None, 'tp')
- w_value: bfloat16 [1024, 512], P(None, 'tp'), may hold values from -0.1875 to 0.1875
- w_out: bfloat16 [1024, 1024], P('tp'), may hold values from -1 to 1
- w_gate: bfloat16 [32, 1024, 512], P('seq', None, 'tp'), as said below
- w_up: bfloat16 [32, 1024, 512], P('seq', None, 'tp'), as said below
- w_down: bfloat16 [32, 512, 1024], P('seq', 'tp'), as said below
Outputs:
- hidden_out: bfloat16 [2048, 1024], P('seq')
- kv_cache: bfloat16 [2048, 2, 512], P('seq', None, 'tp')
Inputs may be any that keep to these rules, and one draw needn't show every extreme that they name: `segment_ids`: segment numbers start at 0, never fall and rise by one at each new segment; no segment is longer than 1536 tokens and one has exactly 1536. `routes`: each row names 8 different experts. In each aligned block of 256 rows no expert is named by more than 128 rows, a bound that some block reaches. Slot s holds the weights of expert s mod 32: w_gate[s] equals w_gate[s mod 32]. w_up[s] equals w_up[s mod 32]. w_down[s] equals w_down[s mod 32].
All inputs are finite; a program needn't handle non-finite values.
Results may differ from a plain program's by a relative error of at most 0.018.
Values may be sent and summed in bfloat16 or wider, within the bound.
A program may use at most 64 MiB of HBM per device.

v0:
```python
import jax
import jax.numpy as jnp
from jax import lax
from jax.sharding import PartitionSpec as P

HEAD_DIM = 64
EXPERTS = 32


EPS = 1e-06
SCORE_SCALE = 0.015625


def normalize(values, gain):
    widened = values.astype(jnp.float32)
    return (
        widened
        * lax.rsqrt(jnp.mean(widened * widened, axis=-1, keepdims=True) + EPS)
        * gain.astype(jnp.float32)
    )


def rotary(tensor, positions):
    half_dim = tensor.shape[-1] // 2
    frequencies = 10000.0 ** (-jnp.arange(half_dim, dtype=jnp.float32) * 2.0 / tensor.shape[-1])
    angles = positions.astype(jnp.float32)[:, None] * frequencies[None, :]
    cosine = jnp.cos(angles)[:, None, :]
    sine_part = jnp.sin(angles)[:, None, :]
    lower_half = tensor[..., :half_dim]
    upper_half = tensor[..., half_dim:]
    return jnp.concatenate(
        [
            lower_half * cosine - upper_half * sine_part,
            upper_half * cosine + lower_half * sine_part,
        ],
        axis=-1,
    )


def segment_positions(segment_ids):
    index_all = jnp.arange(segment_ids.shape[0], dtype=jnp.int32)
    changed = jnp.concatenate([jnp.ones((1,), jnp.bool_), segment_ids[1:] != segment_ids[:-1]])
    starts = lax.cummax(jnp.where(changed, index_all, 0), axis=0)
    return index_all - starts


def per_device(
    hidden,
    segment_ids,
    routes,
    gates,
    norm_attn,
    norm_moe,
    w_query,
    w_key,
    w_value,
    w_out,
    w_gate,
    w_up,
    w_down,
):
    tokens = hidden.shape[0]
    model_width = hidden.shape[1]
    first_row = lax.axis_index("seq") * tokens
    positions = lax.dynamic_slice_in_dim(segment_positions(segment_ids), first_row, tokens)
    own_segs = lax.dynamic_slice_in_dim(segment_ids, first_row, tokens)
    normed = normalize(hidden, norm_attn).astype(jnp.bfloat16)
    query_heads = w_query.shape[1] // HEAD_DIM
    kv_heads = w_key.shape[1] // HEAD_DIM
    group_size = query_heads // kv_heads
    queries = jnp.dot(normed, w_query, preferred_element_type=jnp.float32).reshape(
        tokens, query_heads, HEAD_DIM
    )
    queries = (
        rotary(queries, positions)
        .astype(jnp.bfloat16)
        .reshape(tokens, kv_heads, group_size, HEAD_DIM)
    )
    key_raw = jnp.dot(normed, w_key, preferred_element_type=jnp.float32).reshape(
        tokens, kv_heads, HEAD_DIM
    )
    value_proj = jnp.dot(normed, w_value, preferred_element_type=jnp.float32).astype(jnp.bfloat16)
    kv_cache = jnp.stack(
        [key_raw.reshape(tokens, kv_heads * HEAD_DIM).astype(jnp.bfloat16), value_proj], axis=1
    )
    key_rot = rotary(key_raw, positions).astype(jnp.bfloat16)
    value_heads = value_proj.reshape(tokens, kv_heads, HEAD_DIM)
    query_index = first_row + jnp.arange(tokens, dtype=jnp.int32)
    last_query = first_row + tokens - 1
    lowest_seg = own_segs[0]

    def attend(carried, key_rows, value_rows, key_start, key_segs):
        running_max, weight_sum, accumulated = carried
        scores = (
            jnp.einsum("tkgd,skd->kgts", queries, key_rows, preferred_element_type=jnp.float32)
            * SCORE_SCALE
        )
        key_index = key_start + jnp.arange(key_rows.shape[0], dtype=jnp.int32)
        allowed = (own_segs[:, None] == key_segs[None, :]) & (
            query_index[:, None] >= key_index[None, :]
        )
        masked = jnp.where(allowed, scores, -1e30)
        new_max = jnp.maximum(running_max, jnp.max(masked, axis=-1))
        weights = jnp.where(allowed, jnp.exp(masked - new_max[..., None]), 0.0)
        factor = jnp.exp(running_max - new_max)
        weight_sum = weight_sum * factor + jnp.sum(weights, axis=-1)
        accumulated = accumulated * factor[..., None] + jnp.einsum(
            "kgts,skd->kgtd",
            weights.astype(jnp.bfloat16),
            value_rows,
            preferred_element_type=jnp.float32,
        )
        return (new_max, weight_sum, accumulated)

    start_state = (
        jnp.full((kv_heads, group_size, tokens), -1e30, jnp.float32),
        jnp.zeros((kv_heads, group_size, tokens), jnp.float32),
        jnp.zeros((kv_heads, group_size, tokens, HEAD_DIM), jnp.float32),
    )
    keys_all = lax.all_gather(key_rot, "seq", axis=0, tiled=True)
    values_all = lax.all_gather(value_heads, "seq", axis=0, tiled=True)
    block_total = keys_all.shape[0] // tokens

    def visit_block(block_index, state_now):
        key_start = block_index * tokens
        key_rows = lax.dynamic_slice_in_dim(keys_all, block_index * tokens, tokens)
        value_rows = lax.dynamic_slice_in_dim(values_all, block_index * tokens, tokens)
        key_segs = lax.dynamic_slice_in_dim(segment_ids, key_start, tokens)
        relevant = (key_start <= last_query) & (key_segs[tokens - 1] >= lowest_seg)
        return lax.cond(
            relevant,
            lambda inner: attend(inner, key_rows, value_rows, key_start, key_segs),
            lambda inner: inner,
            state_now,
        )

    running_max, weight_sum, accumulated = lax.fori_loop(0, block_total, visit_block, start_state)
    attended = (
        (accumulated / weight_sum[..., None])
        .transpose(2, 0, 1, 3)
        .reshape(tokens, query_heads * HEAD_DIM)
    )
    attended = attended.astype(jnp.bfloat16)
    partial_out = jnp.dot(attended, w_out, preferred_element_type=jnp.float32)
    attn_mixed = lax.psum(partial_out.astype(jnp.bfloat16), "tp").astype(jnp.float32)
    residual = (hidden.astype(jnp.float32) + attn_mixed).astype(jnp.bfloat16)
    normed_moe = normalize(residual, norm_moe).astype(jnp.bfloat16)
    route_count = routes.shape[1]
    slots_dev = w_gate.shape[0]
    seq_count = lax.axis_size("seq")
    slot_total = slots_dev * seq_count
    copies = slot_total // EXPERTS
    block_rows = tokens // copies
    capacity = 2 * block_rows * route_count // EXPERTS
    copy_of = (jnp.arange(tokens, dtype=jnp.int32) // block_rows)[:, None]
    slot_of = routes + EXPERTS * copy_of
    flat_expert = routes.reshape(copies, block_rows * route_count)
    onehot = (
        flat_expert[:, :, None] == jnp.arange(EXPERTS, dtype=jnp.int32)[None, None, :]
    ).astype(jnp.int32)
    before = jnp.cumsum(onehot, axis=1) - onehot
    slot_rank = jnp.sum(before * onehot, axis=2).reshape(tokens, route_count)
    target = slot_of * capacity + slot_rank
    token_ids = jnp.broadcast_to(
        jnp.arange(tokens, dtype=jnp.int32)[:, None], (tokens, route_count)
    )
    source = (
        jnp.full((slot_total * capacity,), tokens, jnp.int32)
        .at[target.reshape(-1)]
        .set(token_ids.reshape(-1))
    )
    padded_rows = jnp.concatenate([normed_moe, jnp.zeros((1, normed_moe.shape[1]), jnp.bfloat16)])
    outbound = padded_rows[source].reshape(seq_count, slots_dev, capacity, normed_moe.shape[1])
    arrived = lax.all_to_all(outbound, "seq", split_axis=0, concat_axis=0, tiled=True)
    gate_val = jnp.einsum("jsrd,sdf->jsrf", arrived, w_gate, preferred_element_type=jnp.float32)
    up_val = jnp.einsum("jsrd,sdf->jsrf", arrived, w_up, preferred_element_type=jnp.float32)
    activated = (jax.nn.silu(gate_val) * up_val).astype(jnp.bfloat16)
    group_part = jnp.einsum("jsrf,sfd->jsrd", activated, w_down, preferred_element_type=jnp.float32)
    result = group_part.astype(jnp.bfloat16)
    returned = lax.all_to_all(result, "seq", split_axis=0, concat_axis=0, tiled=True).reshape(
        slot_total * capacity, model_width
    )
    picked = returned[target]
    combined = jnp.einsum(
        "tk,tkd->td",
        gates,
        picked,
        preferred_element_type=jnp.float32,
        precision=lax.Precision.HIGHEST,
    )
    expert_sum = lax.psum(combined.astype(jnp.bfloat16), "tp").astype(jnp.float32)
    hidden_out = (residual.astype(jnp.float32) + expert_sum).astype(jnp.bfloat16)
    return (hidden_out, kv_cache)


def solution(mesh):
    return jax.shard_map(
        per_device,
        mesh=mesh,
        in_specs=(
            P("seq", None),
            P(),
            P("seq", None),
            P("seq", None),
            P(),
            P(),
            P(None, "tp"),
            P(None, "tp"),
            P(None, "tp"),
            P("tp", None),
            P("seq", None, "tp"),
            P("seq", None, "tp"),
            P("seq", "tp", None),
        ),
        out_specs=(P("seq", None), P("seq", None, "tp")),
        check_vma=False,
    )
```

profile of v0, /device:TPU:0, one launch (start us, length us, event | category | flops | bytes accessed | tf_op | source)
XLA Modules:
  0.0 420.5 jit_solution(14980686211822164157)
XLA Ops:
  7.2 0.9 slice_compare_fusion
  8.2 0.3 reduce-window.15
  8.6 0.1 slice_reduce_fusion
  8.8 0.8 dynamic_slice.37
  9.6 0.7 convert_element_type.93
  10.3 1.2 fusion.29
  11.5 0.2 multiply_cosine_fusion
  11.7 1.5 fusion.55
  13.3 12.4 %all_gather.6 = bf16[2048,2,64]{0,2,1:T(8,128)(2,1)S(1)} all-gather(bf16[256,2,64]{0,2,1:T(8,128)(2,1)S(1)} %pad_maximum_fusion.2), channel_id=1, replica_groups=mesh['seq'=8,'tp'=4] {'seq'}, dimensions={0}, use_global_device_ids=true | all-gather | bytes 589824 | tf_op jit(solution)/shard_map/all_gather | solution.py:120
  25.7 1.6 fusion.53
  27.4 0.5 slice.41
  27.9 1.5 convolution_convert_fusion.1
  29.4 11.2 %all_gather.7 = bf16[2048,2,64]{0,2,1:T(8,128)(2,1)S(1)} all-gather(bf16[256,2,64]{0,2,1:T(8,128)(2,1)S(1)} %bitcast.113), channel_id=1, replica_groups=mesh['seq'=8,'tp'=4] {'seq'}, dimensions={0}, use_global_device_ids=true | all-gather | bytes 589824 | tf_op jit(solution)/shard_map/all_gather | solution.py:121
  40.7 22.0 %while.18 = (s32[]{:T(128)}, f32[2,2,256]{2,1,0:T(2,128)S(1)}, f32[2,2,256]{2,1,0:T(2,128)S(1)}, f32[2,2,256,64]{2,3,1,0:T(8,128)S(1)}, s32[]{:T(128)}, /*index=...) while((s32[]{:T(128)}, f32[2,2,256]{2,1,0:T(2,128)S(1)}, ...), condition=%wide.region_8.9_spmd.clone, body=%wide.region_3.8_spmd.clone.sunk | while | flops 69798408 | bytes 4270481 | solution.py:137
  40.7 0.8 dynamic_slice.55
  41.5 0.6 slice.78
  43.3 1.1 conditional.3
  43.3 0.1 compare_and_fusion
  43.5 0.4 fusion.57
  43.9 0.2 fusion.5
  44.1 0.3 convolution_add_fusion
  44.5 0.8 dynamic_slice.55
  45.2 0.6 slice.78
  47.1 0.8 dynamic_slice.55
  47.8 0.6 slice.78
  49.7 0.8 dynamic_slice.55
  50.4 0.6 slice.78
  52.3 0.8 dynamic_slice.55
  53.1 0.6 slice.78
  54.9 0.8 dynamic_slice.55
  55.7 0.6 slice.78
  57.5 0.8 dynamic_slice.55
  58.3 0.6 slice.78
  60.1 0.8 dynamic_slice.55
  60.9 0.6 slice.78
  62.7 2.2 convolution_convert_fusion
  64.9 0.1 copy.39
  65.2 9.1 %reduce-window.19 = s32[1,32,16,128]{3,2,1,0:T(8,128)S(1)} reduce-window(s32[1,32,16,128]{3,2,1,0:T(8,128)S(1)} %bitcast.109, s32[]{:T(128)} %constant.106.clone.1), window={size=1x1x1x128 pad=0_0x0_0x0_0x127_0}, to_apply=%region_11.12 | reduce-window | flops 8323072 | bytes 524292 | tf_op jit(solution)/shard_map/reduce-window.2
  74.3 0.1 slice.63
  74.5 0.2 copy.40
  74.8 0.2 reduce-window.24
  75.0 0.1 broadcast.207
  75.4 0.1 copy.43
  75.6 0.1 reshape.298
  75.8 8.1 %scatter_custom_fusion = s32[4096]{0:T(1024)S(1)} fusion(s32[2048]{0:T(1024)S(1)} %bitcast.119, s32[2048]{0:T(1024)S(1)} %reshape.322, s32[]{:T(128)} %constant.116.clone.1), kind=kCustom, calls=%fused_computation.83 | custom fusion | bytes 16388 | tf_op jit(solution)/shard_map/scatter | solution.py:170
  83.9 26.4 %all-reduce.4.cloned.1.call-done = bf16[256,1024]{1,0:T(8,128)(2,1)} async-done(((bf16[256,1024]{1,0:T(8,128)(2,1)}), bf16[256,1024]{1,0:T(8,128)(2,1)}) %all-reduce.4.cloned.1.call-update) | async-done | bytes 524304 | tf_op jit(solution)/shard_map/psum | solution.py:145
  110.3 1.3 fusion.33
  111.6 1.2 fusion.35
  112.9 18.3 %gather_fusion = bf16[4096,1024]{1,0:T(8,128)(2,1)} fusion(bf16[257,1024]{1,0:T(8,128)(2,1)S(1)} %concatenate.27, s32[4096]{0:T(1024)S(1)} %fusion.46), kind=kCustom, calls=%fused_computation | custom fusion | bytes 16793600 | tf_op jit(solution)/shard_map/gather | solution.py:173
  131.2 97.9 %all_to_all.10 = bf16[8,4,128,1024]{3,2,1,0:T(8,128)(2,1)S(1)} all-to-all(bf16[8,4,128,1024]{3,2,1,0:T(8,128)(2,1)} %bitcast.107), channel_id=1, replica_groups=mesh['seq'=8,'tp'=4] {'seq'}, dimensions={0} | all-to-all | bytes 16777216 | tf_op jit(solution)/shard_map/all_to_all | solution.py:174
  229.1 3.2 copy-done.1
  232.3 3.7 fusion.19
  236.0 9.3 %convert_bitcast_fusion = bf16[8,4,128,1024]{3,2,0,1:T(8,128)(2,1)} fusion(bf16[4,128,1024]{2,1,0:T(8,128)(2,1)S(1)} %copy-done, f32[4,8,128,128]{3,2,1,0:T(8,128)} %fusion.19, bf16[8,4,128,1024]{3,2,1,0:T(8,128)(2,1)} %copy-done.1, bf16[4,1024,128]{2,1,0:T(8,128)(2,1)} %param.28), kind=kOutput, calls=%fused_computation.26 | convolution fusion | flops 2154823680 | bytes 20971520 | tf_op jit(solution)/shard_map/jsrf,sfd->jsrd/dot_general | solution.py:178
  245.3 8.2 %copy.46 = bf16[8,4,128,1024]{3,2,1,0:T(8,128)(2,1)} copy(bf16[8,4,128,1024]{3,2,0,1:T(8,128)(2,1)} %convert_bitcast_fusion) | data formatting | bytes 16777216 | tf_op jit(solution)/shard_map/convert_element_type | solution.py:179
  253.5 5.1 %all-to-all-start.1 = ((bf16[8,4,128,1024]{3,2,1,0:T(8,128)(2,1)}), bf16[8,4,128,1024]{3,2,1,0:T(8,128)(2,1)}, u32[]{:S(2)}, u32[]{:S(2)}) async-start(bf16[8,4,128,1024]{3,2,1,0:T(8,128)(2,1)} %copy.46), calls=%async_computation.1 | async-start | bytes 16777216 | tf_op jit(solution)/shard_map/all_to_all | solution.py:180
  258.7 0.1 copy.47
  258.9 0.1 copy.55
  259.1 93.6 %all-to-all-done.1 = bf16[8,4,128,1024]{3,2,1,0:T(8,128)(2,1)} async-done(((bf16[8,4,128,1024]{3,2,1,0:T(8,128)(2,1)}), bf16[8,4,128,1024]{3,2,1,0:T(8,128)(2,1)}, u32[]{:S(2)}, u32[]{:S(2)}) %all-to-all-start.1) | async-done | bytes 8388640 | tf_op jit(solution)/shard_map/all_to_all | solution.py:180
  352.7 15.5 %gather_fusion.1 = bf16[2048,1024]{1,0:T(8,128)(2,1)} fusion(bf16[4096,1024]{1,0:T(8,128)(2,1)} %bitcast.30, s32[2048]{0:T(1024)S(1)} %broadcast_clamp_fusion), kind=kCustom, calls=%fused_computation.1 | custom fusion | bytes 8396800 | tf_op jit(solution)/shard_map/gather | solution.py:183
  368.2 5.9 %fusion.21 = bf16[256,1,1024]{2,1,0:T(2,128)(2,1)S(1)} fusion(f32[256,8,1]{1,2,0:T(1,128)S(1)} %copy.55, bf16[2048,1024]{1,0:T(8,128)(2,1)} %gather_fusion.1), kind=kOutput, calls=%fused_computation.31 | convolution fusion | flops 25165824 | bytes 4726784 | tf_op jit(solution)/shard_map/tk,tkd->td/dot_general | solution.py:184
  374.0 1.0 copy.67
  375.0 0.8 copy.48
  375.8 35.8 %all-reduce.6.cloned.1.call-done = bf16[256,1024]{1,0:T(8,128)(2,1)} async-done(((bf16[256,1024]{1,0:T(8,128)(2,1)}), bf16[256,1024]{1,0:T(8,128)(2,1)}) %all-reduce.6.cloned.1.call-update) | async-done | bytes 524304 | tf_op jit(solution)/shard_map/psum | solution.py:191
  411.6 2.1 fusion.36
  (76 shorter events, 1.7 us)
Async XLA Ops:
  7.2 228.8 %copy-start = (bf16[4,128,1024]{2,1,0:T(8,128)(2,1)S(1)}, bf16[4,128,1024]{2,1,0:T(8,128)(2,1)}, u32[]{:S(2)}) copy-start(bf16[4,128,1024]{2,1,0:T(8,128)(2,1)} %param.29) | copy-start | bytes 3145732
  7.2 103.1 %all-reduce.4.cloned.1.call-start = ((), (), s32[]{:S(2)}) async-start(), calls=%async_computation.2 | async-start | bytes 1048576 | tf_op jit(solution)/shard_map/psum | solution.py:145
  40.6 24.3 %copy-start.4 = (s32[256,8]{0,1:T(8,128)S(1)}, s32[256,8]{0,1:T(8,128)}, u32[]{:S(2)}) copy-start(s32[256,8]{0,1:T(8,128)} %param.19) | copy-start | bytes 24580
  40.7 33.9 %copy-start.6 = (bf16[1024]{0:T(1024)(128)(2,1)S(1)}, bf16[1024]{0:T(1024)(128)(2,1)}, u32[]{:S(2)}) copy-start(bf16[1024]{0:T(1024)(128)(2,1)} %param.22) | copy-start | bytes 6148
  40.7 69.6 %copy-start.2 = (bf16[256,1024]{1,0:T(8,128)(2,1)S(1)}, bf16[256,1024]{1,0:T(8,128)(2,1)}, u32[]{:S(2)}) copy-start(bf16[256,1024]{1,0:T(8,128)(2,1)} %param.17) | copy-start | bytes 1572868
  131.2 101.1 %copy-start.7 = (bf16[4,1024,128]{2,1,0:T(8,128)(2,1)S(1)}, bf16[4,1024,128]{2,1,0:T(8,128)(2,1)}, u32[]{:S(2)}) copy-start(bf16[4,1024,128]{2,1,0:T(8,128)(2,1)} %param.27) | copy-start | bytes 3145732
  229.1 3.2 copy-start.1
  253.5 5.4 %copy-start.5 = (f32[256,8]{0,1:T(8,128)S(1)}, f32[256,8]{0,1:T(8,128)}, u32[]{:S(2)}) copy-start(f32[256,8]{0,1:T(8,128)} %param.20) | copy-start | bytes 24580
  253.5 99.2 %all-to-all-start.1 = ((bf16[8,4,128,1024]{3,2,1,0:T(8,128)(2,1)}), bf16[8,4,128,1024]{3,2,1,0:T(8,128)(2,1)}, u32[]{:S(2)}, u32[]{:S(2)}) async-start(bf16[8,4,128,1024]{3,2,1,0:T(8,128)(2,1)} %copy.46), calls=%async_computation.1 | async-start | bytes 16777216 | tf_op jit(solution)/shard_map/all_to_all | solution.py:180
  258.6 153.0 %all-reduce.6.cloned.1.call-start = ((), (), s32[]{:S(2)}) async-start(), calls=%async_computation.3 | async-start | bytes 1048576 | tf_op jit(solution)/shard_map/psum | solution.py:191
  368.1 43.4 %copy-start.3 = (bf16[256,1024]{1,0:T(8,128)(2,1)S(1)}, bf16[256,1024]{1,0:T(8,128)(2,1)}, u32[]{:S(2)}) copy-start(bf16[256,1024]{1,0:T(8,128)(2,1)} %all-reduce.4.cloned.1.call-done) | copy-start | bytes 1572868
Sparse Core Ops, SparseCore 0:
  65.0 45.2 all-reduce.3
  375.1 36.4 all-reduce.5
where the time goes:
time: 421 us
  waiting for transfers between devices  156 us (37%)
  blocking collectives  122 us (29%)
  local copies, waits for them, and re-layouts  69.4 us (16%)
  matrix products  26.3 us (6%)
  other arithmetic  18.1 us (4%)
  between operations  14.4 us (3%)
  loops' own time  9.84 us (2%)
  starting transfers between devices  5.17 us (1%)
    all_to_all x1, blocking collectives, per_device(): lax.all_to_all(outbound, 'seq', split_axis=0, concat_axis=0, tiled=True)  97.9 us
    all_to_all x1, waiting for transfers between devices, per_device(): lax.all_to_all(result, 'seq', split_axis=0, concat_axis=0, tiled=True)  93.6 us
    psum x1, waiting for transfers between devices, per_device(): lax.psum(combined.astype(jnp.bfloat16), 'tp').astype(jnp.float32)  35.8 us
    psum x1, waiting for transfers between devices, per_device(): lax.psum(partial_out.astype(jnp.bfloat16), 'tp').astype(jnp.float32)  26.4 us
    gather x1, local copies, waits for them, and re-layouts, per_device(): padded_rows[source]  18.3 us
    gather x1, local copies, waits for them, and re-layouts, per_device(): picked = returned[target]  15.5 us
    all_gather x1, blocking collectives, per_device(): keys_all = lax.all_gather(key_rot, 'seq', axis=0, tiled=True)  12.4 us
    all_gather x1, blocking collectives, per_device(): values_all = lax.all_gather(value_heads, 'seq', axis=0, tiled=True)  11.2 us
  transfers between devices with their start and end apart: 3, of which 3 were waited for; matrix products, arithmetic and copies ran while one was open for 5% of the time, Pallas kernels for 0%

commit v1 on v0

--- a/solution.py
+++ b/solution.py
@@ -44,7 +44,7 @@
     return index_all - starts
 
 
-def per_device(
+def per_device_routed(
     hidden,
     segment_ids,
     routes,
@@ -193,9 +193,117 @@
     return (hidden_out, kv_cache)
 
 
+def attention_inputs(hidden, segment_ids, norm_attn, w_query, w_key, w_value):
+    tokens = hidden.shape[0]
+    first_row = lax.axis_index("seq") * tokens
+    own_segs = lax.dynamic_slice_in_dim(segment_ids, first_row, tokens)
+    query_index = first_row + jnp.arange(tokens, dtype=jnp.int32)
+    starts = jnp.sum((segment_ids[None, :] < own_segs[:, None]).astype(jnp.int32), axis=1)
+    positions = query_index - starts
+    normed = normalize(hidden, norm_attn).astype(jnp.bfloat16)
+    query_heads = w_query.shape[1] // HEAD_DIM
+    kv_heads = w_key.shape[1] // HEAD_DIM
+    queries = jnp.dot(normed, w_query, preferred_element_type=jnp.float32)
+    key_raw = jnp.dot(normed, w_key, preferred_element_type=jnp.float32)
+    value_proj = jnp.dot(normed, w_value, preferred_element_type=jnp.float32).astype(jnp.bfloat16)
+    kv_cache = jnp.stack([key_raw.astype(jnp.bfloat16), value_proj], axis=1)
+    queries = rotary(queries.reshape(tokens, query_heads, HEAD_DIM), positions)
+    key_rot = rotary(key_raw.reshape(tokens, kv_heads, HEAD_DIM), positions)
+    queries = queries.astype(jnp.bfloat16)
+    key_rot = key_rot.astype(jnp.bfloat16).reshape(tokens, kv_heads * HEAD_DIM)
+    return queries, key_rot, value_proj, kv_cache, own_segs, query_index, starts
+
+
+def attend_all(queries, keys_all, values_all, query_index, starts):
+    tokens, query_heads, _ = queries.shape
+    total = keys_all.shape[0]
+    kv_heads = keys_all.shape[1] // HEAD_DIM
+    grouped = queries.reshape(tokens, kv_heads, query_heads // kv_heads, HEAD_DIM)
+    keys = keys_all.reshape(total, kv_heads, HEAD_DIM)
+    values = values_all.reshape(total, kv_heads, HEAD_DIM)
+    scores = (
+        jnp.einsum("tkgd,skd->kgts", grouped, keys, preferred_element_type=jnp.float32)
+        * SCORE_SCALE
+    )
+    key_index = jnp.arange(total, dtype=jnp.int32)
+    allowed = (key_index[None, :] <= query_index[:, None]) & (
+        key_index[None, :] >= starts[:, None]
+    )
+    masked = jnp.where(allowed, scores, -1e30)
+    top = jnp.max(masked, axis=-1, keepdims=True)
+    weights = jnp.where(allowed, jnp.exp(masked - top), 0.0)
+    weight_sum = jnp.sum(weights, axis=-1)
+    mixed = jnp.einsum(
+        "kgts,skd->kgtd",
+        weights.astype(jnp.bfloat16),
+        values,
+        preferred_element_type=jnp.float32,
+    )
+    attended = (mixed / weight_sum[..., None]).transpose(2, 0, 1, 3)
+    return attended.reshape(tokens, query_heads * HEAD_DIM).astype(jnp.bfloat16)
+
+
+def expert_gates(routes, gates, experts):
+    hit = routes[:, :, None] == jnp.arange(experts, dtype=jnp.int32)[None, None, :]
+    return jnp.sum(jnp.where(hit, gates[:, :, None], 0.0), axis=1)
+
+
+def per_device(
+    hidden,
+    segment_ids,
+    routes,
+    gates,
+    norm_attn,
+    norm_moe,
+    w_query,
+    w_key,
+    w_value,
+    w_out,
+    w_gate,
+    w_up,
+    w_down,
+):
+    tokens, width = hidden.shape
+    slots, _, units = w_gate.shape
+    part = tokens // lax.axis_size("tp")
+    queries, key_rot, value_proj, kv_cache, own_segs, query_index, starts = attention_inputs(
+        hidden, segment_ids, norm_attn, w_query, w_key, w_value
+    )
+    table = lax.all_gather(expert_gates(routes, gates, EXPERTS), "seq", axis=0, tiled=True)
+    own_gates = lax.dynamic_slice_in_dim(table, lax.axis_index("seq") * slots, slots, axis=1)
+    kv = lax.all_gather(
+        jnp.concatenate([key_rot, value_proj], axis=1), "seq", axis=0, tiled=True
+    )
+    half = kv.shape[1] // 2
+    attended = attend_all(queries, kv[:, :half], kv[:, half:], query_index, starts)
+    partial_out = jnp.dot(attended, w_out, preferred_element_type=jnp.float32)
+    mixed = lax.psum_scatter(
+        partial_out.astype(jnp.bfloat16), "tp", scatter_dimension=0, tiled=True
+    )
+    own_part = lax.dynamic_slice_in_dim(hidden, lax.axis_index("tp") * part, part)
+    residual = (own_part.astype(jnp.float32) + mixed.astype(jnp.float32)).astype(jnp.bfloat16)
+    normed = normalize(residual, norm_moe).astype(jnp.bfloat16)
+    rows = lax.all_gather(normed, ("seq", "tp"), axis=0, tiled=True)
+    total = jnp.zeros((rows.shape[0], width), jnp.float32)
+    for slot in range(slots):
+        gate_val = jnp.dot(rows, w_gate[slot], preferred_element_type=jnp.float32)
+        up_val = jnp.dot(rows, w_up[slot], preferred_element_type=jnp.float32)
+        scale = own_gates[:, slot : slot + 1]
+        act = jnp.where(scale > 0, jax.nn.silu(gate_val) * up_val * scale, 0.0)
+        total = total + jnp.dot(
+            act.astype(jnp.bfloat16), w_down[slot], preferred_element_type=jnp.float32
+        )
+    summed = lax.psum_scatter(
+        total.astype(jnp.bfloat16), ("seq", "tp"), scatter_dimension=0, tiled=True
+    )
+    out_part = (residual.astype(jnp.float32) + summed.astype(jnp.float32)).astype(jnp.bfloat16)
+    return lax.all_gather(out_part, "tp", axis=0, tiled=True), kv_cache
+
+
 def solution(mesh):
+    whole_rows = mesh.shape["seq"] <= 8
     return jax.shard_map(
-        per_device,
+        per_device if whole_rows else per_device_routed,
         mesh=mesh,
         in_specs=(
             P("seq", None),

time: 421 us -> 357 us (0.85)
  blocking collectives: 122 us -> 25.3 us
  waiting for transfers between devices: 156 us -> 244 us
  local copies, waits for them, and re-layouts: 69.4 us -> 3.68 us
  matrix products: 26.3 us -> 62.2 us
  other arithmetic: 18.1 us -> 7.43 us
  loops' own time: 9.84 us -> 0 us
  starting transfers between devices: 5.17 us -> 0.16 us
    reduce_scatter x0 -> x2, waiting for transfers between devices: none -> 167 us  [the longest x1 146 us: per_device(): lax.psum_scatter(total.astype(jnp.bfloat16), ('seq', 'tp'), scatter_dimen...]
    all_to_all x1 -> x0, blocking collectives: 97.9 us -> none  [per_device(): lax.all_to_all(outbound, 'seq', split_axis=0, concat_axis=0, tiled=True)]
    all_to_all x1 -> x0, waiting for transfers between devices: 93.6 us -> none  [per_device(): lax.all_to_all(result, 'seq', split_axis=0, concat_axis=0, tiled=True)]
    all_gather x0 -> x2, waiting for transfers between devices: none -> 76.7 us  [the longest x1 52.5 us: per_device(): rows = lax.all_gather(normed, ('seq', 'tp'), axis=0, tiled=True)]
    psum x2 -> x0, waiting for transfers between devices: 62.2 us -> none  [the longest x1 35.8 us: per_device(): lax.psum(combined.astype(jnp.bfloat16), 'tp').astype(jnp.float32)]
    gather x2 -> x0, local copies, waits for them, and re-layouts: 33.7 us -> none  [the longest x1 18.3 us: per_device(): padded_rows[source]]
    dot_general x8 -> x12, matrix products: 24.2 us -> 55.6 us  [the longest x4 37.4 us: per_device(): jnp.dot(act.astype(jnp.bfloat16), w_down[slot], preferred_element_type=jn...]
    another operation x9 -> x0, loops' own time: 9.84 us -> none  [the longest x1 9.71 us: per_device(): lax.fori_loop(0, block_total, visit_block, start_state)]
  transfers between devices with their start and end apart: 3 -> 4, of which waited for: 3 -> 4; matrix products, arithmetic and copies ran while one was open for 5% -> 1% of each run, Pallas kernels for 0% -> 0%
where the time goes in v1:
time: 357 us
  waiting for transfers between devices  244 us (68%)
  matrix products  62.2 us (17%)
  blocking collectives  25.3 us (7%)
  between operations  14 us (4%)
  other arithmetic  7.43 us (2%)
  local copies, waits for them, and re-layouts  3.68 us (1%)
    reduce_scatter x1, waiting for transfers between devices, per_device(): lax.psum_scatter(total.astype(jnp.bfloat16), ('seq', 'tp'), scatter_dimen...  146 us
    all_gather x1, waiting for transfers between devices, per_device(): rows = lax.all_gather(normed, ('seq', 'tp'), axis=0, tiled=True)  52.5 us
    dot_general x4, matrix products, per_device(): jnp.dot(act.astype(jnp.bfloat16), w_down[slot], preferred_element_type=jn...  37.4 us
    all_gather x1, waiting for transfers between devices, per_device(): lax.all_gather(jnp.concatenate([key_rot, value_proj], axis=1), 'seq', axi...  24.2 us
    reduce_scatter x1, waiting for transfers between devices, per_device(): lax.psum_scatter(partial_out.astype(jnp.bfloat16), 'tp', scatter_dimensio...  21.7 us
    all_gather x1, blocking collectives, per_device(): return (lax.all_gather(out_part, 'tp', axis=0, tiled=True), kv_cache)  16 us
    dot_general x4, matrix products, per_device(): gate_val = jnp.dot(rows, w_gate[slot], preferred_element_type=jnp.float32)  10.5 us
    all_gather x1, blocking collectives, per_device(): lax.all_gather(expert_gates(routes, gates, EXPERTS), 'seq', axis=0, tiled...  9.31 us
  transfers between devices with their start and end apart: 4, of which 4 were waited for; matrix products, arithmetic and copies ran while one was open for 1% of the time, Pallas kernels for 0%

profile of v1, /device:TPU:0, one launch (start us, length us, event | category | flops | bytes accessed | tf_op | source)
XLA Modules:
  0.0 356.9 jit_solution(17814941312209962755)
XLA Ops:
  7.2 0.0 copy-start
  7.2 0.0 all-gather.3.cloned.1.call-start
  7.2 0.8 dynamic_slice.10
  8.1 1.0 convert_reduce_fusion
  9.1 1.2 fusion.34
  10.3 0.7 convert_element_type.88
  11.0 1.5 convolution_convert_fusion.1
  12.5 1.5 fusion.126
  14.0 0.2 multiply_cosine_fusion
  14.3 0.7 pad_maximum_fusion
  15.0 0.0 all-gather.3.cloned.1.call-update
  15.0 0.0 reduce-scatter.3.cloned.1.call-start
  15.0 1.6 fusion.123
  16.7 0.5 fusion.21
  17.2 24.2 %all-gather.3.cloned.1.call-done = bf16[2048,256]{0,1:T(8,128)(2,1)} async-done(((bf16[256,256]{0,1:T(8,128)(2,1)}), bf16[2048,256]{0,1:T(8,128)(2,1)}) %all-gather.3.cloned.1.call-update) | async-done | bytes 1048592 | tf_op jit(solution)/shard_map/all_gather | solution.py:274
  41.4 1.3 fusion.128
  42.7 5.5 %fusion.129 = (f32[2,2,256]{2,1,0:T(2,128)S(1)}, bf16[2,2,256,2048]{2,3,1,0:T(8,128)(2,1)}) fusion(bf16[2048,2,64,1]{0,2,3,1:T(8,128)(2,1)S(1)} %bitcast.101, pred[256,2048]{0,1:T(8,128)(4,1)S(1)} %fusion.21, bf16[256,2,2,32]{0,3,2,1:T(8,128)(2,1)S(1)} %bitcast.106, bf16[256,2,2,32]{0,3,2,1:T(8,128)(2,1)S(1)} %bitcast.105), kind=kOutput, calls=%fused_computation.153 | convolution fusion | flops 281282560 | bytes 5378048 | tf_op jit(solution)/shard_map/sub | solution.py:234
  48.2 0.0 copy-start.5
  48.2 0.0 copy-start.3
  48.2 0.0 copy-start.4
  48.2 3.1 fusion.31
  51.2 0.0 copy-done
  51.2 1.1 convolution_convert_fusion
  52.4 0.0 reduce-scatter.3.cloned.1.call-update
  52.4 0.0 all-gather.5.cloned.1.call-start
  52.4 0.0 copy-done.5
  52.5 21.7 %reduce-scatter.3.cloned.1.call-done = bf16[64,1024]{1,0:T(8,128)(2,1)} async-done(((bf16[256,1024]{1,0:T(8,128)(2,1)}), bf16[64,1024]{1,0:T(8,128)(2,1)}) %reduce-scatter.3.cloned.1.call-update) | async-done | bytes 131088 | tf_op jit(solution)/shard_map/reduce_scatter | solution.py:280
  74.2 1.1 fusion.68
  75.3 0.8 fusion.70
  76.1 0.0 all-gather.5.cloned.1.call-update
  76.1 0.0 reduce-scatter.5.cloned.1.call-start
  76.2 0.0 copy-done.3
  76.2 0.0 copy-done.4
  76.2 9.3 %all_gather.13 = f32[2048,32]{0,1:T(8,128)S(1)} all-gather(f32[256,32]{0,1:T(8,128)S(1)} %select_reduce_fusion), channel_id=1, replica_groups=mesh['seq'=8,'tp'=4] {'seq'}, dimensions={0}, use_global_device_ids=true | all-gather | bytes 294912 | tf_op jit(solution)/shard_map/all_gather | solution.py:272
  85.5 0.1 compare_reduce_fusion
  85.7 52.5 %all-gather.5.cloned.1.call-done = bf16[2048,1024]{1,0:T(8,128)(2,1)} async-done(((bf16[64,1024]{1,0:T(8,128)(2,1)}), bf16[2048,1024]{1,0:T(8,128)(2,1)}) %all-gather.5.cloned.1.call-update) | async-done | bytes 4194320 | tf_op jit(solution)/shard_map/all_gather | solution.py:286
  138.2 0.0 copy-start.1
  138.2 3.6 %fusion.75 = f32[2048,128]{1,0:T(8,128)S(1)} fusion(bf16[2048,1024]{1,0:T(8,128)(2,1)} %all-gather.5.cloned.1.call-done, bf16[4,1024,128]{2,1,0:T(8,128)(2,1)} %param.23), kind=kOutput, calls=%fused_computation.84 | convolution fusion | flops 536870912 | bytes 5505024 | tf_op jit(solution)/shard_map/dot_general | solution.py:289
  141.8 0.0 copy-done.1
  141.8 0.0 copy-start.2
  141.8 2.3 fusion.80
  144.2 0.0 copy-done.2
  144.2 2.3 fusion.85
  146.4 2.3 fusion.90
  148.8 8.2 %fusion.24 = f32[2048,1024]{1,0:T(8,128)} fusion(bf16[2048,1024]{1,0:T(8,128)(2,1)} %all-gather.5.cloned.1.call-done, f32[2048,128]{1,0:T(8,128)} %fusion.90, f32[2048]{0:T(1024)S(1)} %bitcast.109, pred[2048]{0:T(1024)(128)(4,1)S(1)} %get-tuple-element.26, bf16[4,128,1024]{2,1,0:T(8,128)(2,1)} %param.25, bf16[4,1024,128]{2,1,0:T(8,128)(2,1)} %param.24), kind=kOutput, calls=%fused_computation.36 | convolution fusion | flops 1075838976 | bytes 14166016 | tf_op jit(solution)/shard_map/dot_general | solution.py:293
  156.9 8.1 %fusion.23 = f32[2048,1024]{1,0:T(8,128)} fusion(bf16[2048,1024]{1,0:T(8,128)(2,1)} %all-gather.5.cloned.1.call-done, f32[2048,128]{1,0:T(8,128)} %fusion.85, f32[2048]{0:T(1024)S(1)} %bitcast.108, pred[2048]{0:T(1024)(128)(4,1)S(1)} %get-tuple-element.24, bf16[4,128,1024]{2,1,0:T(8,128)(2,1)} %param.25, bf16[4,1024,128]{2,1,0:T(8,128)(2,1)} %param.24), kind=kOutput, calls=%fused_computation.35 | convolution fusion | flops 1075838976 | bytes 14166016 | tf_op jit(solution)/shard_map/dot_general | solution.py:293
  165.1 8.0 %fusion.22 = f32[2048,1024]{1,0:T(8,128)} fusion(bf16[2048,1024]{1,0:T(8,128)(2,1)} %all-gather.5.cloned.1.call-done, f32[2048,128]{1,0:T(8,128)S(1)} %fusion.80, f32[2048]{0:T(1024)S(1)} %bitcast.107, pred[2048]{0:T(1024)(128)(4,1)S(1)} %get-tuple-element.22, bf16[4,128,1024]{2,1,0:T(8,128)(2,1)} %param.25, bf16[4,1024,128]{2,1,0:T(8,128)(2,1)} %param.24), kind=kOutput, calls=%fused_computation.34 | convolution fusion | flops 1075838976 | bytes 14166016 | tf_op jit(solution)/shard_map/dot_general | solution.py:293
  173.0 13.1 %add_convert_fusion = bf16[2048,1024]{1,0:T(8,128)(2,1)} fusion(f32[2048,1024]{1,0:T(8,128)} %fusion.22, f32[2048,1024]{1,0:T(8,128)} %fusion.24, f32[2048,1024]{1,0:T(8,128)} %fusion.23, bf16[2048,1024]{1,0:T(8,128)(2,1)} %all-gather.5.cloned.1.call-done, f32[2048,128]{1,0:T(8,128)S(1)} %fusion.75, f32[2048]{0:T(1024)S(1)} %bitcast.110, ...), kind=kOutput, calls=%fused_computation.2 | convolution fusion | flops 1084227584 | bytes 35137536 | tf_op jit(solution)/shard_map/dot_general | solution.py:293
  186.1 0.0 reduce-scatter.5.cloned.1.call-update
  186.2 0.8 copy.24
  187.0 145.7 %reduce-scatter.5.cloned.1.call-done = bf16[64,1024]{1,0:T(8,128)(2,1)} async-done(((bf16[2048,1024]{1,0:T(8,128)(2,1)}), bf16[64,1024]{1,0:T(8,128)(2,1)}) %reduce-scatter.5.cloned.1.call-update) | async-done | bytes 131088 | tf_op jit(solution)/shard_map/reduce_scatter | solution.py:296
  332.6 0.9 fusion.71
  333.6 16.0 %all_gather.15 = bf16[256,1024]{1,0:T(8,128)(2,1)S(1)} all-gather(bf16[64,1024]{1,0:T(8,128)(2,1)S(1)} %fusion.71), channel_id=1, replica_groups=mesh['seq'=8,'tp'=4] {'tp'}, dimensions={0}, use_global_device_ids=true | all-gather | bytes 655360 | tf_op jit(solution)/shard_map/all_gather | solution.py:300
  349.6 0.8 copy.29
  (12 shorter events, 0.2 us)
Async XLA Ops:
  7.2 44.1 %copy-start = (bf16[256,1024]{1,0:T(8,128)(2,1)S(1)}, bf16[256,1024]{1,0:T(8,128)(2,1)}, u32[]{:S(2)}) copy-start(bf16[256,1024]{1,0:T(8,128)(2,1)} %param.22) | copy-start | bytes 1572868
  7.2 34.2 %all-gather.3.cloned.1.call-start = ((), (), s32[]{:S(2)}) async-start(), calls=%async_computation.2 | async-start | bytes 1179648 | tf_op jit(solution)/shard_map/all_gather | solution.py:274
  15.0 59.2 %reduce-scatter.3.cloned.1.call-start = ((), (), s32[]{:S(2)}) async-start(), calls=%async_computation.3 | async-start | bytes 655360 | tf_op jit(solution)/shard_map/reduce_scatter | solution.py:280
  48.2 4.3 %copy-start.5 = (bf16[1024]{0:T(1024)(128)(2,1)S(1)}, bf16[1024]{0:T(1024)(128)(2,1)}, u32[]{:S(2)}) copy-start(bf16[1024]{0:T(1024)(128)(2,1)} %param.18) | copy-start | bytes 6148
  48.2 28.0 %copy-start.3 = (f32[256,8]{0,1:T(8,128)S(1)}, f32[256,8]{0,1:T(8,128)}, u32[]{:S(2)}) copy-start(f32[256,8]{0,1:T(8,128)} %param.16) | copy-start | bytes 24580
  48.2 28.0 %copy-start.4 = (s32[256,8]{0,1:T(8,128)S(1)}, s32[256,8]{0,1:T(8,128)}, u32[]{:S(2)}) copy-start(s32[256,8]{0,1:T(8,128)} %param.15) | copy-start | bytes 24580
  52.4 85.8 %all-gather.5.cloned.1.call-start = ((), (), s32[]{:S(2)}) async-start(), calls=%async_computation.4 | async-start | bytes 4325376 | tf_op jit(solution)/shard_map/all_gather | solution.py:286
  76.1 256.5 %reduce-scatter.5.cloned.1.call-start = ((), (), s32[]{:S(2)}) async-start(), calls=%async_computation.5 | async-start | bytes 4325376 | tf_op jit(solution)/shard_map/reduce_scatter | solution.py:296
  138.2 3.6 %copy-start.1 = (bf16[2048,1024]{1,0:T(8,128)(2,1)S(1)}, bf16[2048,1024]{1,0:T(8,128)(2,1)}, u32[]{:S(2)}) copy-start(bf16[2048,1024]{1,0:T(8,128)(2,1)} %all-gather.5.cloned.1.call-done) | copy-start | bytes 12582916
  141.8 2.3 copy-start.2
Sparse Core Ops, SparseCore 0:
  15.1 26.2 all-gather.2
  52.5 21.6 reduce-scatter.2
  77.8 60.4 all-gather.4
  186.3 146.3 reduce-scatter.4

commit v2 on v1

--- a/solution.py
+++ b/solution.py
@@ -1,6 +1,8 @@
 import jax
 import jax.numpy as jnp
 from jax import lax
+from jax.experimental import pallas as pl
+from jax.experimental.pallas import tpu as pltpu
 from jax.sharding import PartitionSpec as P
 
 HEAD_DIM = 64
@@ -248,6 +250,259 @@
     return jnp.sum(jnp.where(hit, gates[:, :, None], 0.0), axis=1)
 
 
+def flip(seq_index, mask):
+    bits = [seq_index // 4, (seq_index // 2) % 2, seq_index % 2]
+    bits = [1 - bit if (mask >> (2 - n)) & 1 else bit for n, bit in enumerate(bits)]
+    return bits[0] * 4 + bits[1] * 2 + bits[2]
+
+
+CORE, XDIR, YDIR = 1, 2, 4
+
+
+def experts_kernel(
+    normed_ref, residual_ref, gates_ref, wg_hbm, wu_hbm, wd_hbm, out_ref,
+    rows, weights, downs, act, parts, from_core, first, second, from_tp,
+    weight_sem, send_sem, row_sem, core_sem, first_sem, second_sem, tp_sem, out_sem,
+):
+    me, tp = lax.axis_index("seq"), lax.axis_index("tp")
+    n_tp = rows.shape[1]
+    block = rows.shape[2]
+    slots = weights.shape[0]
+    units = weights.shape[2] // 2
+    width = rows.shape[3]
+    seq_peer = {mask: (flip(me, mask), tp) for mask in (CORE, XDIR, YDIR)}
+    tp_peer = {k: (me, (tp + k) % n_tp) for k in range(1, n_tp)}
+
+    loads = []
+    for n in range(slots):
+        for half, source in ((0, wg_hbm), (1, wu_hbm)):
+            loads.append(
+                pltpu.make_async_copy(
+                    source.at[n],
+                    weights.at[n, :, pl.ds(half * units, units)],
+                    weight_sem.at[2 * n + half],
+                )
+            )
+    loads.append(pltpu.make_async_copy(wd_hbm, downs, weight_sem.at[2 * slots]))
+    for load in loads:
+        load.start()
+
+    barrier = pltpu.get_barrier_semaphore()
+    peers = list(seq_peer.values()) + list(tp_peer.values())
+    for peer in peers:
+        pl.semaphore_signal(
+            barrier, inc=1, device_id=peer, device_id_type=pl.DeviceIdType.MESH
+        )
+    pl.semaphore_wait(barrier, len(peers))
+
+    sent = []
+
+    def send(source, target, sem, peer):
+        copy = pltpu.make_async_remote_copy(
+            src_ref=source,
+            dst_ref=target,
+            send_sem=send_sem.at[len(sent)],
+            recv_sem=sem,
+            device_id=peer,
+            device_id_type=pl.DeviceIdType.MESH,
+        )
+        copy.start()
+        sent.append(copy)
+
+    def arrived(target, sem):
+        pltpu.make_async_remote_copy(
+            src_ref=target,
+            dst_ref=target,
+            send_sem=send_sem.at[0],
+            recv_sem=sem,
+            device_id=seq_peer[CORE],
+            device_id_type=pl.DeviceIdType.MESH,
+        ).wait_recv()
+
+    def pass_on(mask, k, way, source=None):
+        source = rows.at[mask, k] if source is None else source
+        send(source, rows.at[mask ^ way, k], row_sem.at[mask ^ way, k], seq_peer[way])
+
+    def take(mask, k):
+        arrived(rows.at[mask, k], row_sem.at[mask, k])
+
+    rows[0, 0] = normed_ref[...]
+    for k in (2, 1, 3):
+        back = n_tp - k
+        send(normed_ref, rows.at[0, back], row_sem.at[0, back], tp_peer[k])
+    for way in (XDIR, YDIR, CORE):
+        pass_on(0, 0, way, normed_ref)
+
+    def handle_sides(k):
+        take(XDIR, k)
+        if k >= 2:
+            pass_on(XDIR, k, YDIR)
+        take(YDIR, k)
+        if k < 2:
+            pass_on(YDIR, k, XDIR)
+        pass_on(XDIR, k, CORE)
+        pass_on(YDIR, k, CORE)
+
+    def compute(mask):
+        group = rows[mask].reshape(n_tp * block, width)
+        seq_row = flip(me, mask) * (n_tp * block)
+        gate = jnp.concatenate(
+            [
+                gates_ref[pl.ds(pl.multiple_of(seq_row + ((tp + k) % n_tp) * block, block), block), :]
+                for k in range(n_tp)
+            ],
+            axis=0,
+        )
+        for n in range(slots):
+            both = jnp.dot(group, weights[n], preferred_element_type=jnp.float32)
+            gate_val, up_val = both[:, :units], both[:, units:]
+            scale = gate[:, n : n + 1]
+            value = gate_val / (1.0 + jnp.exp(-gate_val)) * up_val * scale
+            act[:, n * units : (n + 1) * units] = jnp.where(scale > 0, value, 0.0).astype(
+                jnp.bfloat16
+            )
+        step = 256
+        for column in range(0, width, step):
+            piece = jnp.dot(
+                act[...],
+                downs[:, column : column + step],
+                preferred_element_type=jnp.float32,
+            ).astype(jnp.bfloat16)
+            for k in range(n_tp):
+                parts[mask, k, :, column : column + step] = piece[k * block : (k + 1) * block]
+
+    def give_core(mask):
+        send(parts.at[mask], from_core.at[mask // 2], core_sem.at[mask // 2], seq_peer[CORE])
+
+    def add(mask, k, extra):
+        parts[mask, k] = (
+            parts[mask, k].astype(jnp.float32) + extra.astype(jnp.float32)
+        ).astype(jnp.bfloat16)
+
+    def add_core(mask):
+        arrived(from_core.at[mask // 2], core_sem.at[mask // 2])
+        for k in range(n_tp):
+            add(mask, k, from_core[mask // 2, k])
+
+    for k in (1, 3, 2):
+        take(0, k)
+        for way in (XDIR, YDIR, CORE):
+            pass_on(0, k, way)
+    handle_sides(0)
+    handle_sides(1)
+    for load in loads:
+        load.wait()
+    compute(0)
+    handle_sides(3)
+    handle_sides(2)
+    for k in range(n_tp):
+        take(CORE, k)
+    compute(1)
+    give_core(1)
+    compute(2)
+    for k in range(n_tp):
+        take(XDIR + CORE, k)
+    compute(3)
+    give_core(3)
+    for k in range(n_tp):
+        take(YDIR + XDIR, k)
+        pass_on(YDIR + XDIR, k, CORE)
+    for k in range(n_tp):
+        take(YDIR + CORE, k)
+    compute(5)
+    give_core(5)
+    compute(4)
+    for k in range(n_tp):
+        take(YDIR + XDIR + CORE, k)
+    compute(7)
+    give_core(7)
+    compute(6)
+
+    early = ((XDIR, YDIR, (1, 0)), (YDIR, XDIR, (2, 3)))
+
+    def give_first(mask, way, ks):
+        for k in ks:
+            slot = 0 if mask == way else 1
+            send(parts.at[mask, k], first.at[slot, k], first_sem.at[slot, k], seq_peer[way])
+
+    for way, other, ks in early:
+        add_core(way)
+        give_first(way, way, ks)
+    add_core(XDIR + YDIR)
+    for way, other, ks in early:
+        give_first(XDIR + YDIR, way, ks)
+    add_core(0)
+    for way, other, ks in early:
+        for k in ks:
+            arrived(first.at[1, k], first_sem.at[1, k])
+            add(other, k, first[1, k])
+            send(parts.at[other, k], second.at[k], second_sem.at[k], seq_peer[other])
+    for k in (2, 1, 3, 0):
+        arrived(first.at[0, k], first_sem.at[0, k])
+        add(0, k, first[0, k])
+    for k in (2, 1, 3, 0):
+        arrived(second.at[k], second_sem.at[k])
+        add(0, k, second[k])
+        if k:
+            back = n_tp - k
+            send(parts.at[0, k], from_tp.at[back], tp_sem.at[back], tp_peer[k])
+    total = residual_ref[...].astype(jnp.float32) + parts[0, 0].astype(jnp.float32)
+    for k in (1, 3, 2):
+        arrived(from_tp.at[k], tp_sem.at[k])
+        total = total + from_tp[k].astype(jnp.float32)
+    own = out_ref.at[pl.ds(pl.multiple_of(tp * block, block), block)]
+    own[...] = total.astype(jnp.bfloat16)
+    for k in (2, 1, 3):
+        send(own, own, out_sem.at[n_tp - k], tp_peer[k])
+    for k in (1, 3, 2):
+        start = pl.multiple_of(((tp + k) % n_tp) * block, block)
+        arrived(out_ref.at[pl.ds(start, block)], out_sem.at[k])
+    for copy in sent:
+        copy.wait_send()
+
+
+def run_experts(normed, residual, own_gates, w_gate, w_up, w_down):
+    block, width = normed.shape
+    n_tp = lax.axis_size("tp")
+    n_seq = lax.axis_size("seq")
+    slots, _, units = w_gate.shape
+    bf16 = jnp.bfloat16
+    flops = 2 * own_gates.shape[0] * slots * width * units * 3
+    return pl.pallas_call(
+        experts_kernel,
+        out_shape=jax.ShapeDtypeStruct((n_tp * block, width), bf16),
+        in_specs=[pl.BlockSpec(memory_space=pltpu.VMEM)] * 3
+        + [pl.BlockSpec(memory_space=pl.ANY)] * 3,
+        out_specs=pl.BlockSpec(memory_space=pltpu.VMEM),
+        scratch_shapes=[
+            pltpu.VMEM((n_seq, n_tp, block, width), bf16),
+            pltpu.VMEM((slots, width, 2 * units), bf16),
+            pltpu.VMEM((slots * units, width), bf16),
+            pltpu.VMEM((n_tp * block, slots * units), bf16),
+            pltpu.VMEM((n_seq, n_tp, block, width), bf16),
+            pltpu.VMEM((n_seq // 2, n_tp, block, width), bf16),
+            pltpu.VMEM((2, n_tp, block, width), bf16),
+            pltpu.VMEM((n_tp, block, width), bf16),
+            pltpu.VMEM((n_tp, block, width), bf16),
+            pltpu.SemaphoreType.DMA((2 * slots + 1,)),
+            pltpu.SemaphoreType.DMA((64,)),
+            pltpu.SemaphoreType.DMA((n_seq, n_tp)),
+            pltpu.SemaphoreType.DMA((n_seq // 2,)),
+            pltpu.SemaphoreType.DMA((2, n_tp)),
+            pltpu.SemaphoreType.DMA((n_tp,)),
+            pltpu.SemaphoreType.DMA((n_tp,)),
+            pltpu.SemaphoreType.DMA((n_tp,)),
+        ],
+        compiler_params=pltpu.CompilerParams(
+            collective_id=0, has_side_effects=True, vmem_limit_bytes=40 * 1024 * 1024
+        ),
+        cost_estimate=pl.CostEstimate(
+            flops=flops, bytes_accessed=4 * 1024 * 1024, transcendentals=0
+        ),
+        name="experts",
+    )(normed, residual, own_gates, w_gate, w_up, w_down.reshape(slots * units, width))
+
+
 def per_device(
     hidden,
     segment_ids,
@@ -264,18 +519,26 @@
     w_down,
 ):
     tokens, width = hidden.shape
-    slots, _, units = w_gate.shape
+    slots = w_gate.shape[0]
     part = tokens // lax.axis_size("tp")
     queries, key_rot, value_proj, kv_cache, own_segs, query_index, starts = attention_inputs(
         hidden, segment_ids, norm_attn, w_query, w_key, w_value
     )
-    table = lax.all_gather(expert_gates(routes, gates, EXPERTS), "seq", axis=0, tiled=True)
-    own_gates = lax.dynamic_slice_in_dim(table, lax.axis_index("seq") * slots, slots, axis=1)
-    kv = lax.all_gather(
-        jnp.concatenate([key_rot, value_proj], axis=1), "seq", axis=0, tiled=True
-    )
-    half = kv.shape[1] // 2
-    attended = attend_all(queries, kv[:, :half], kv[:, half:], query_index, starts)
+    table = expert_gates(routes, gates, EXPERTS)
+    high = table.astype(jnp.bfloat16)
+    low = (table - high.astype(jnp.float32)).astype(jnp.bfloat16)
+    kv_width = key_rot.shape[1]
+    gathered = lax.all_gather(
+        jnp.concatenate([key_rot, value_proj, high, low], axis=1), "seq", axis=0, tiled=True
+    )
+    keys_all, values_all = gathered[:, :kv_width], gathered[:, kv_width : 2 * kv_width]
+    first_column = 2 * kv_width + lax.axis_index("seq") * slots
+    own_gates = lax.dynamic_slice_in_dim(gathered, first_column, slots, axis=1).astype(
+        jnp.float32
+    ) + lax.dynamic_slice_in_dim(gathered, first_column + EXPERTS, slots, axis=1).astype(
+        jnp.float32
+    )
+    attended = attend_all(queries, keys_all, values_all, query_index, starts)
     partial_out = jnp.dot(attended, w_out, preferred_element_type=jnp.float32)
     mixed = lax.psum_scatter(
         partial_out.astype(jnp.bfloat16), "tp", scatter_dimension=0, tiled=True
@@ -283,25 +546,12 @@
     own_part = lax.dynamic_slice_in_dim(hidden, lax.axis_index("tp") * part, part)
     residual = (own_part.astype(jnp.float32) + mixed.astype(jnp.float32)).astype(jnp.bfloat16)
     normed = normalize(residual, norm_moe).astype(jnp.bfloat16)
-    rows = lax.all_gather(normed, ("seq", "tp"), axis=0, tiled=True)
-    total = jnp.zeros((rows.shape[0], width), jnp.float32)
-    for slot in range(slots):
-        gate_val = jnp.dot(rows, w_gate[slot], preferred_element_type=jnp.float32)
-        up_val = jnp.dot(rows, w_up[slot], preferred_element_type=jnp.float32)
-        scale = own_gates[:, slot : slot + 1]
-        act = jnp.where(scale > 0, jax.nn.silu(gate_val) * up_val * scale, 0.0)
-        total = total + jnp.dot(
-            act.astype(jnp.bfloat16), w_down[slot], preferred_element_type=jnp.float32
-        )
-    summed = lax.psum_scatter(
-        total.astype(jnp.bfloat16), ("seq", "tp"), scatter_dimension=0, tiled=True
-    )
-    out_part = (residual.astype(jnp.float32) + summed.astype(jnp.float32)).astype(jnp.bfloat16)
-    return lax.all_gather(out_part, "tp", axis=0, tiled=True), kv_cache
+    hidden_out = run_experts(normed, residual, own_gates, w_gate, w_up, w_down)
+    return hidden_out, kv_cache
 
 
 def solution(mesh):
-    whole_rows = mesh.shape["seq"] <= 8
+    whole_rows = mesh.shape["seq"] == 8 and mesh.shape["tp"] == 4
     return jax.shard_map(
         per_device if whole_rows else per_device_routed,
         mesh=mesh,

time: 357 us -> 162 us (0.45)
  waiting for transfers between devices: 244 us -> 46.8 us
  Pallas kernels: 0 us -> 72.2 us
  matrix products: 62.2 us -> 13.1 us
  blocking collectives: 25.3 us -> 0 us
    reduce_scatter x1 -> x0, waiting for transfers between devices: 146 us -> none  [per_device(): lax.psum_scatter(total.astype(jnp.bfloat16), ('seq', 'tp'), scatter_dimen...]
    pallas_call x0 -> x1, Pallas kernels: none -> 72.2 us  [run_experts(): pl.pallas_call(experts_kernel, out_shape=jax.ShapeDtypeStruct((n_tp * blo...]
    all_gather x2 -> x1, waiting for transfers between devices: 76.7 us -> 27.5 us  [per_device(): lax.all_gather(jnp.concatenate([key_rot, value_proj, high, low], axis=1),...]
    dot_general x8 -> x0, matrix products: 47.9 us -> none  [the longest x4 37.4 us: per_device(): jnp.dot(act.astype(jnp.bfloat16), w_down[slot], preferred_element_type=jn...]
    all_gather x2 -> x0, blocking collectives: 25.3 us -> none  [the longest x1 16 us: per_device(): return (lax.all_gather(out_part, 'tp', axis=0, tiled=True), kv_cache)]
  transfers between devices with their start and end apart: 4 -> 2, of which waited for: 4 -> 2; matrix products, arithmetic and copies ran while one was open for 1% -> 2% of each run, Pallas kernels for 0% -> 0%
where the time goes in v2:
time: 162 us
  Pallas kernels  72.2 us (45%)
  waiting for transfers between devices  46.8 us (29%)
  between operations  14.3 us (9%)
  matrix products  13.1 us (8%)
  other arithmetic  8.15 us (5%)
  local copies, waits for them, and re-layouts  6.95 us (4%)
    pallas_call x1, Pallas kernels, run_experts(): pl.pallas_call(experts_kernel, out_shape=jax.ShapeDtypeStruct((n_tp * blo...  72.2 us
    all_gather x1, waiting for transfers between devices, per_device(): lax.all_gather(jnp.concatenate([key_rot, value_proj, high, low], axis=1),...  27.5 us
    reduce_scatter x1, waiting for transfers between devices, per_device(): lax.psum_scatter(partial_out.astype(jnp.bfloat16), 'tp', scatter_dimensio...  19.3 us
    sub x1, matrix products, attend_all(): weights = jnp.where(allowed, jnp.exp(masked - top), 0.0)  5.49 us
    unnamed x16, local copies, waits for them, and re-layouts  4.06 us
  transfers between devices with their start and end apart: 2, of which 2 were waited for; matrix products, arithmetic and copies ran while one was open for 2% of the time, Pallas kernels for 0%

profile of v2, /device:TPU:0, one launch (start us, length us, event | category | flops | bytes accessed | tf_op | source)
XLA Modules:
  0.0 161.5 jit_solution(9613130799496399360)
XLA Ops:
  7.2 0.0 copy-start
  7.2 0.0 copy-start.4
  7.2 0.0 copy-start.6
  7.2 0.0 all-gather.2.cloned.1.call-start
  7.3 0.9 select_reduce_fusion
  8.1 0.1 copy.47
  8.2 0.8 dynamic_slice.13
  9.0 1.0 convert_reduce_fusion
  10.0 1.2 fusion.19
  11.3 0.7 convert_element_type.81
  12.0 0.1 copy.49
  12.1 1.5 convolution_convert_fusion.1
  13.6 1.5 fusion.35
  15.1 0.2 multiply_cosine_fusion
  15.3 0.1 copy.48
  15.5 0.8 pad_maximum_fusion
  16.2 0.0 all-gather.2.cloned.1.call-update
  16.3 0.0 reduce-scatter.2.cloned.1.call-start
  16.3 0.0 copy-done.4
  16.3 0.0 copy-done.6
  16.3 0.5 fusion.32
  16.8 0.5 fusion.9
  17.3 27.5 %all-gather.2.cloned.1.call-done = bf16[2048,320]{1,0:T(8,128)(2,1)} async-done(((bf16[256,320]{1,0:T(8,128)(2,1)}), bf16[2048,320]{1,0:T(8,128)(2,1)}) %all-gather.2.cloned.1.call-update) | async-done | bytes 1310736 | tf_op jit(solution)/shard_map/all_gather | solution.py:531
  44.8 1.3 fusion.37
  46.1 0.2 copy.50
  46.3 0.2 copy.51
  46.5 5.5 %fusion.38 = (f32[2,2,256]{2,1,0:T(2,128)S(1)}, bf16[2,2,256,2048]{2,3,1,0:T(8,128)(2,1)}) fusion(bf16[2048,2,64,1]{0,2,3,1:T(8,128)(2,1)S(1)} %bitcast.51, pred[256,2048]{0,1:T(8,128)(4,1)S(1)} %fusion.9, bf16[256,2,2,32]{0,3,2,1:T(8,128)(2,1)S(1)} %bitcast.58, bf16[256,2,2,32]{0,3,2,1:T(8,128)(2,1)S(1)} %bitcast.57), kind=kOutput, calls=%fused_computation.58 | convolution fusion | flops 281282560 | bytes 5378048 | tf_op jit(solution)/shard_map/sub | solution.py:236
  52.0 0.0 copy-start.5
  52.0 0.0 copy-start.1
  52.0 3.1 %fusion.16 = bf16[256,2,2,64]{0,3,2,1:T(8,128)(2,1)S(1)} fusion(bf16[2048,2,64,1]{0,2,3,1:T(8,128)(2,1)S(1)} %bitcast.49, bf16[2,2,256,2048]{2,3,1,0:T(8,128)(2,1)} %get-tuple-element.21, f32[256,2,2]{0,2,1:T(2,128)S(1)} %bitcast.59), kind=kOutput, calls=%fused_computation.19 | convolution fusion | flops 268566528 | bytes 4853760 | tf_op jit(solution)/shard_map/kgts,skd->kgtd/dot_general | solution.py:238
  55.1 0.0 copy-done
  55.1 1.1 convolution_convert_fusion
  56.2 0.0 reduce-scatter.2.cloned.1.call-update
  56.3 0.1 copy.53
  56.4 0.0 copy-done.5
  56.4 0.8 copy.54
  57.2 1.6 convert_add_fusion.gates_ref
  58.8 19.3 %reduce-scatter.2.cloned.1.call-done = bf16[64,1024]{1,0:T(8,128)(2,1)} async-done(((bf16[256,1024]{1,0:T(8,128)(2,1)}), bf16[64,1024]{1,0:T(8,128)(2,1)}) %reduce-scatter.2.cloned.1.call-update) | async-done | bytes 131088 | tf_op jit(solution)/shard_map/reduce_scatter | solution.py:543
  78.1 1.1 fusion.22
  79.1 0.1 fusion.24.normed_ref
  79.3 0.0 copy-done.1
  79.3 0.0 copy-start.2
  79.3 1.2 copy-done.2
  80.5 0.0 copy-start.3
  80.5 1.2 copy-done.3
  81.7 72.2 %experts.1 = bf16[256,1024]{1,0:T(8,128)(2,1)S(1)} custom-call(bf16[64,1024]{1,0:T(8,128)(2,1)S(1)} %fusion.24.normed_ref, bf16[64,1024]{1,0:T(8,128)(2,1)S(1)} %get-tuple-element.11.residual_ref, f32[2048,4]{1,0:T(8,128)S(1)} %convert_add_fusion.gates_ref, bf16[4,1024,128]{2,1,0:T(8,128)(2,1)S(1)} %copy-done.1, bf16[4,1024,128]{2,1,0:T(8,128)(2,1)S(1)} %copy-done.2, ...), custom_call_target="tpu_custom_call" | custom-call | flops 6442450944 | bytes 4194304 | tf_op jit(solution)/shard_map/experts/pallas_call | solution.py:471
  153.9 0.8 copy.60
  (11 shorter events, 0.1 us)
Async XLA Ops:
  7.2 48.0 %copy-start = (bf16[256,1024]{1,0:T(8,128)(2,1)S(1)}, bf16[256,1024]{1,0:T(8,128)(2,1)}, u32[]{:S(2)}) copy-start(bf16[256,1024]{1,0:T(8,128)(2,1)} %param.22) | copy-start | bytes 1572868
  7.2 9.1 %copy-start.4 = (bf16[256,1024]{1,0:T(8,128)(2,1)S(1)}, bf16[256,1024]{1,0:T(8,128)(2,1)}, u32[]{:S(2)}) copy-start(bf16[256,1024]{1,0:T(8,128)(2,1)} %param.13) | copy-start | bytes 1572868
  7.2 9.1 %copy-start.6 = (bf16[1024,256]{1,0:T(8,128)(2,1)S(1)}, bf16[1024,256]{1,0:T(8,128)(2,1)}, u32[]{:S(2)}) copy-start(bf16[1024,256]{1,0:T(8,128)(2,1)} %param.19) | copy-start | bytes 1572868
  7.2 37.6 %all-gather.2.cloned.1.call-start = ((), (), s32[]{:S(2)}) async-start(), calls=%async_computation.1 | async-start | bytes 1769472 | tf_op jit(solution)/shard_map/all_gather | solution.py:531
  16.3 61.8 %reduce-scatter.2.cloned.1.call-start = ((), (), s32[]{:S(2)}) async-start(), calls=%async_computation.2 | async-start | bytes 655360 | tf_op jit(solution)/shard_map/reduce_scatter | solution.py:543
  52.0 4.4 %copy-start.5 = (bf16[1024]{0:T(1024)(128)(2,1)S(1)}, bf16[1024]{0:T(1024)(128)(2,1)}, u32[]{:S(2)}) copy-start(bf16[1024]{0:T(1024)(128)(2,1)} %param.18) | copy-start | bytes 6148
  52.0 27.3 %copy-start.1 = (bf16[4,1024,128]{2,1,0:T(8,128)(2,1)S(1)}, bf16[4,1024,128]{2,1,0:T(8,128)(2,1)}, u32[]{:S(2)}) copy-start(bf16[4,1024,128]{2,1,0:T(8,128)(2,1)} %wg_hbm.1) | copy-start | bytes 3145732
  79.3 1.2 copy-start.2
  80.5 1.2 copy-start.3
Sparse Core Ops, SparseCore 0:
  16.4 28.3 all-gather.1
  56.4 21.6 reduce-scatter.1

commit v3 on v2

--- a/solution.py
+++ b/solution.py
@@ -216,38 +216,15 @@
     return queries, key_rot, value_proj, kv_cache, own_segs, query_index, starts
 
 
-def attend_all(queries, keys_all, values_all, query_index, starts):
-    tokens, query_heads, _ = queries.shape
-    total = keys_all.shape[0]
-    kv_heads = keys_all.shape[1] // HEAD_DIM
-    grouped = queries.reshape(tokens, kv_heads, query_heads // kv_heads, HEAD_DIM)
-    keys = keys_all.reshape(total, kv_heads, HEAD_DIM)
-    values = values_all.reshape(total, kv_heads, HEAD_DIM)
-    scores = (
-        jnp.einsum("tkgd,skd->kgts", grouped, keys, preferred_element_type=jnp.float32)
-        * SCORE_SCALE
-    )
-    key_index = jnp.arange(total, dtype=jnp.int32)
-    allowed = (key_index[None, :] <= query_index[:, None]) & (
-        key_index[None, :] >= starts[:, None]
-    )
-    masked = jnp.where(allowed, scores, -1e30)
-    top = jnp.max(masked, axis=-1, keepdims=True)
-    weights = jnp.where(allowed, jnp.exp(masked - top), 0.0)
-    weight_sum = jnp.sum(weights, axis=-1)
-    mixed = jnp.einsum(
-        "kgts,skd->kgtd",
-        weights.astype(jnp.bfloat16),
-        values,
-        preferred_element_type=jnp.float32,
-    )
-    attended = (mixed / weight_sum[..., None]).transpose(2, 0, 1, 3)
-    return attended.reshape(tokens, query_heads * HEAD_DIM).astype(jnp.bfloat16)
-
-
 def expert_gates(routes, gates, experts):
     hit = routes[:, :, None] == jnp.arange(experts, dtype=jnp.int32)[None, None, :]
     return jnp.sum(jnp.where(hit, gates[:, :, None], 0.0), axis=1)
+
+
+def normalize_rows(values, gain):
+    widened = values.astype(jnp.float32)
+    mean = jnp.mean(widened * widened, axis=-1, keepdims=True)
+    return widened * lax.rsqrt(mean + EPS) * gain.astype(jnp.float32)
 
 
 def flip(seq_index, mask):
@@ -259,8 +236,11 @@
 CORE, XDIR, YDIR = 1, 2, 4
 
 
-def experts_kernel(
-    normed_ref, residual_ref, gates_ref, wg_hbm, wu_hbm, wd_hbm, out_ref,
+def layer_kernel(
+    query_ref, kv_ref, table_ref, starts_ref, hidden_ref, norm_ref, wo_ref,
+    wg_hbm, wu_hbm, wd_hbm, out_ref,
+    kv, table, top, norm_sum, mixed, partial_out, from_heads, residual, normed_ref,
+    kv_sem, table_sem, heads_sem,
     rows, weights, downs, act, parts, from_core, first, second, from_tp,
     weight_sem, send_sem, row_sem, core_sem, first_sem, second_sem, tp_sem, out_sem,
 ):
@@ -319,49 +299,166 @@
             device_id_type=pl.DeviceIdType.MESH,
         ).wait_recv()
 
-    def pass_on(mask, k, way, source=None):
-        source = rows.at[mask, k] if source is None else source
-        send(source, rows.at[mask ^ way, k], row_sem.at[mask ^ way, k], seq_peer[way])
-
-    def take(mask, k):
-        arrived(rows.at[mask, k], row_sem.at[mask, k])
-
+    def spread(buffer, sems, parts_of):
+        def go(mask, k, way):
+            send(buffer.at[mask, k], buffer.at[mask ^ way, k], sems.at[mask ^ way, k], seq_peer[way])
+
+        def take(mask, k):
+            arrived(buffer.at[mask, k], sems.at[mask, k])
+
+        def sides(k):
+            take(XDIR, k)
+            if k >= parts_of // 2:
+                go(XDIR, k, YDIR)
+            take(YDIR, k)
+            if k < parts_of // 2:
+                go(YDIR, k, XDIR)
+            go(XDIR, k, CORE)
+            go(YDIR, k, CORE)
+
+        return go, take, sides
+
+    halves = (0, 1)
+    kv_go, kv_take, kv_sides = spread(kv, kv_sem, 2)
+    table_go, table_take, table_sides = spread(table, table_sem, 2)
+    half = kv.shape[2]
+    for k in halves:
+        kv[0, k] = kv_ref[k * half : (k + 1) * half, :]
+        table[0, k] = table_ref[k * half : (k + 1) * half, :]
+    for k in halves:
+        for way in (XDIR, YDIR, CORE):
+            kv_go(0, k, way)
+    for k in halves:
+        for way in (XDIR, YDIR, CORE):
+            table_go(0, k, way)
+
+    tokens = 2 * half
+    kv_width = kv.shape[3] // 2
+    heads = query_ref.shape[0] // tokens
+    top[...] = jnp.full(top.shape, -1e30, jnp.float32)
+    norm_sum[...] = jnp.zeros(norm_sum.shape, jnp.float32)
+    mixed[...] = jnp.zeros(mixed.shape, jnp.float32)
+
+    def attend(mask):
+        block_kv = kv[mask].reshape(tokens, 2 * kv_width)
+        keys, values = block_kv[:, :kv_width], block_kv[:, kv_width:]
+        query_index = me * tokens + lax.broadcasted_iota(jnp.int32, (tokens, tokens), 0)
+        key_index = flip(me, mask) * tokens + lax.broadcasted_iota(
+            jnp.int32, (tokens, tokens), 1
+        )
+        allowed = (key_index <= query_index) & (key_index >= starts_ref[...])
+
+        for head in range(heads):
+            span = pl.ds(head * tokens, tokens)
+            scores = (
+                lax.dot_general(
+                    query_ref[span, :],
+                    keys,
+                    (((1,), (1,)), ((), ())),
+                    preferred_element_type=jnp.float32,
+                )
+                * SCORE_SCALE
+            )
+            masked = jnp.where(allowed, scores, -1e30)
+            old_top = top[span, :]
+            new_top = jnp.maximum(old_top, jnp.max(masked, axis=1, keepdims=True))
+            weights_now = jnp.where(allowed, jnp.exp(masked - new_top), 0.0)
+            factor = jnp.exp(old_top - new_top)
+            top[span, :] = new_top
+            norm_sum[span, :] = norm_sum[span, :] * factor + jnp.sum(
+                weights_now, axis=1, keepdims=True
+            )
+            mixed[span, :] = mixed[span, :] * factor + jnp.dot(
+                weights_now.astype(jnp.bfloat16), values, preferred_element_type=jnp.float32
+            )
+
+    attend(0)
+    for k in halves:
+        kv_sides(k)
+    for k in halves:
+        kv_take(CORE, k)
+    attend(XDIR)
+    attend(YDIR)
+    for k in halves:
+        kv_take(XDIR + YDIR, k)
+        kv_go(XDIR + YDIR, k, CORE)
+    attend(CORE)
+    for k in halves:
+        table_sides(k)
+    attend(XDIR + YDIR)
+    for mask in (XDIR + CORE, YDIR + CORE, XDIR + YDIR + CORE):
+        for k in halves:
+            kv_take(mask, k)
+        attend(mask)
+    for k in halves:
+        table_take(XDIR + YDIR, k)
+        table_go(XDIR + YDIR, k, CORE)
+
+    attended = jnp.concatenate(
+        [
+            (mixed[pl.ds(h * tokens, tokens), :] / norm_sum[pl.ds(h * tokens, tokens), :]).astype(
+                jnp.bfloat16
+            )
+            for h in range(heads)
+        ],
+        axis=1,
+    )
+    step = 256
+    for column in range(0, width, step):
+        partial_out[:, column : column + step] = jnp.dot(
+            attended, wo_ref[:, column : column + step], preferred_element_type=jnp.float32
+        ).astype(jnp.bfloat16)
+
+    def block_rows(k):
+        return pl.ds(pl.multiple_of(((tp + k) % n_tp) * block, block), block)
+
+    for k in (2, 1, 3):
+        back = n_tp - k
+        send(partial_out.at[block_rows(k)], from_heads.at[back], heads_sem.at[back], tp_peer[k])
+    summed = partial_out[block_rows(0), :].astype(jnp.float32)
+    for k in (1, 3, 2):
+        arrived(from_heads.at[k], heads_sem.at[k])
+        summed = summed + from_heads[k].astype(jnp.float32)
+    added = hidden_ref[block_rows(0), :].astype(jnp.float32) + summed
+    residual[...] = added.astype(jnp.bfloat16)
+    normed_ref[...] = normalize_rows(residual[...], norm_ref[...]).astype(jnp.bfloat16)
+
+    pass_on, take, handle_sides = spread(rows, row_sem, n_tp)
     rows[0, 0] = normed_ref[...]
     for k in (2, 1, 3):
         back = n_tp - k
-        send(normed_ref, rows.at[0, back], row_sem.at[0, back], tp_peer[k])
+        send(rows.at[0, 0], rows.at[0, back], row_sem.at[0, back], tp_peer[k])
     for way in (XDIR, YDIR, CORE):
-        pass_on(0, 0, way, normed_ref)
-
-    def handle_sides(k):
-        take(XDIR, k)
-        if k >= 2:
-            pass_on(XDIR, k, YDIR)
-        take(YDIR, k)
-        if k < 2:
-            pass_on(YDIR, k, XDIR)
-        pass_on(XDIR, k, CORE)
-        pass_on(YDIR, k, CORE)
+        pass_on(0, 0, way)
+    for mask in (CORE, XDIR + CORE, YDIR + CORE, XDIR + YDIR + CORE):
+        for k in halves:
+            table_take(mask, k)
 
     def compute(mask):
         group = rows[mask].reshape(n_tp * block, width)
-        seq_row = flip(me, mask) * (n_tp * block)
         gate = jnp.concatenate(
             [
-                gates_ref[pl.ds(pl.multiple_of(seq_row + ((tp + k) % n_tp) * block, block), block), :]
+                table[
+                    mask,
+                    ((tp + k) % n_tp) // 2,
+                    pl.ds(pl.multiple_of(((tp + k) % 2) * block, block), block),
+                    :,
+                ]
                 for k in range(n_tp)
             ],
             axis=0,
-        )
+        ).astype(jnp.float32)
+        lane = lax.broadcasted_iota(jnp.int32, gate.shape, 1)
         for n in range(slots):
             both = jnp.dot(group, weights[n], preferred_element_type=jnp.float32)
             gate_val, up_val = both[:, :units], both[:, units:]
-            scale = gate[:, n : n + 1]
+            column = me * slots + n
+            chosen = (lane == column) | (lane == column + EXPERTS)
+            scale = jnp.sum(jnp.where(chosen, gate, 0.0), axis=1, keepdims=True)
             value = gate_val / (1.0 + jnp.exp(-gate_val)) * up_val * scale
             act[:, n * units : (n + 1) * units] = jnp.where(scale > 0, value, 0.0).astype(
                 jnp.bfloat16
             )
-        step = 256
         for column in range(0, width, step):
             piece = jnp.dot(
                 act[...],
@@ -446,7 +543,7 @@
         if k:
             back = n_tp - k
             send(parts.at[0, k], from_tp.at[back], tp_sem.at[back], tp_peer[k])
-    total = residual_ref[...].astype(jnp.float32) + parts[0, 0].astype(jnp.float32)
+    total = residual[...].astype(jnp.float32) + parts[0, 0].astype(jnp.float32)
     for k in (1, 3, 2):
         arrived(from_tp.at[k], tp_sem.at[k])
         total = total + from_tp[k].astype(jnp.float32)
@@ -461,31 +558,45 @@
         copy.wait_send()
 
 
-def run_experts(normed, residual, own_gates, w_gate, w_up, w_down):
-    block, width = normed.shape
+def run_layer(queries, kv, table, starts, hidden, norm_moe, w_out, w_gate, w_up, w_down):
+    tokens, width = hidden.shape
     n_tp = lax.axis_size("tp")
     n_seq = lax.axis_size("seq")
+    block = tokens // n_tp
     slots, _, units = w_gate.shape
-    bf16 = jnp.bfloat16
-    flops = 2 * own_gates.shape[0] * slots * width * units * 3
+    lanes = queries.shape[1]
+    bf16, f32 = jnp.bfloat16, jnp.float32
+    flops = 2 * n_seq * tokens * slots * width * units * 3
     return pl.pallas_call(
-        experts_kernel,
-        out_shape=jax.ShapeDtypeStruct((n_tp * block, width), bf16),
-        in_specs=[pl.BlockSpec(memory_space=pltpu.VMEM)] * 3
+        layer_kernel,
+        out_shape=jax.ShapeDtypeStruct((tokens, width), bf16),
+        in_specs=[pl.BlockSpec(memory_space=pltpu.VMEM)] * 7
         + [pl.BlockSpec(memory_space=pl.ANY)] * 3,
         out_specs=pl.BlockSpec(memory_space=pltpu.VMEM),
         scratch_shapes=[
+            pltpu.VMEM((n_seq, 2, tokens // 2, kv.shape[1]), bf16),
+            pltpu.VMEM((n_seq, 2, tokens // 2, table.shape[1]), bf16),
+            pltpu.VMEM((queries.shape[0], 1), f32),
+            pltpu.VMEM((queries.shape[0], 1), f32),
+            pltpu.VMEM((queries.shape[0], lanes), f32),
+            pltpu.VMEM((tokens, width), bf16),
+            pltpu.VMEM((n_tp, block, width), bf16),
+            pltpu.VMEM((block, width), bf16),
+            pltpu.VMEM((block, width), bf16),
+            pltpu.SemaphoreType.DMA((n_seq, 2)),
+            pltpu.SemaphoreType.DMA((n_seq, 2)),
+            pltpu.SemaphoreType.DMA((n_tp,)),
             pltpu.VMEM((n_seq, n_tp, block, width), bf16),
             pltpu.VMEM((slots, width, 2 * units), bf16),
             pltpu.VMEM((slots * units, width), bf16),
-            pltpu.VMEM((n_tp * block, slots * units), bf16),
+            pltpu.VMEM((tokens, slots * units), bf16),
             pltpu.VMEM((n_seq, n_tp, block, width), bf16),
             pltpu.VMEM((n_seq // 2, n_tp, block, width), bf16),
             pltpu.VMEM((2, n_tp, block, width), bf16),
             pltpu.VMEM((n_tp, block, width), bf16),
             pltpu.VMEM((n_tp, block, width), bf16),
             pltpu.SemaphoreType.DMA((2 * slots + 1,)),
-            pltpu.SemaphoreType.DMA((64,)),
+            pltpu.SemaphoreType.DMA((112,)),
             pltpu.SemaphoreType.DMA((n_seq, n_tp)),
             pltpu.SemaphoreType.DMA((n_seq // 2,)),
             pltpu.SemaphoreType.DMA((2, n_tp)),
@@ -494,13 +605,24 @@
             pltpu.SemaphoreType.DMA((n_tp,)),
         ],
         compiler_params=pltpu.CompilerParams(
-            collective_id=0, has_side_effects=True, vmem_limit_bytes=40 * 1024 * 1024
+            collective_id=0, has_side_effects=True, vmem_limit_bytes=48 * 1024 * 1024
         ),
         cost_estimate=pl.CostEstimate(
             flops=flops, bytes_accessed=4 * 1024 * 1024, transcendentals=0
         ),
-        name="experts",
-    )(normed, residual, own_gates, w_gate, w_up, w_down.reshape(slots * units, width))
+        name="layer",
+    )(
+        queries,
+        kv,
+        table,
+        starts,
+        hidden,
+        norm_moe,
+        w_out,
+        w_gate,
+        w_up,
+        w_down.reshape(slots * units, width),
+    )
 
 
 def per_device(
@@ -519,34 +641,38 @@
     w_down,
 ):
     tokens, width = hidden.shape
-    slots = w_gate.shape[0]
-    part = tokens // lax.axis_size("tp")
     queries, key_rot, value_proj, kv_cache, own_segs, query_index, starts = attention_inputs(
         hidden, segment_ids, norm_attn, w_query, w_key, w_value
     )
     table = expert_gates(routes, gates, EXPERTS)
     high = table.astype(jnp.bfloat16)
     low = (table - high.astype(jnp.float32)).astype(jnp.bfloat16)
-    kv_width = key_rot.shape[1]
-    gathered = lax.all_gather(
-        jnp.concatenate([key_rot, value_proj, high, low], axis=1), "seq", axis=0, tiled=True
-    )
-    keys_all, values_all = gathered[:, :kv_width], gathered[:, kv_width : 2 * kv_width]
-    first_column = 2 * kv_width + lax.axis_index("seq") * slots
-    own_gates = lax.dynamic_slice_in_dim(gathered, first_column, slots, axis=1).astype(
-        jnp.float32
-    ) + lax.dynamic_slice_in_dim(gathered, first_column + EXPERTS, slots, axis=1).astype(
-        jnp.float32
-    )
-    attended = attend_all(queries, keys_all, values_all, query_index, starts)
-    partial_out = jnp.dot(attended, w_out, preferred_element_type=jnp.float32)
-    mixed = lax.psum_scatter(
-        partial_out.astype(jnp.bfloat16), "tp", scatter_dimension=0, tiled=True
-    )
-    own_part = lax.dynamic_slice_in_dim(hidden, lax.axis_index("tp") * part, part)
-    residual = (own_part.astype(jnp.float32) + mixed.astype(jnp.float32)).astype(jnp.bfloat16)
-    normed = normalize(residual, norm_moe).astype(jnp.bfloat16)
-    hidden_out = run_experts(normed, residual, own_gates, w_gate, w_up, w_down)
+    fill = jnp.zeros((tokens, 128 - 2 * EXPERTS), jnp.bfloat16)
+    table = jnp.concatenate([high, low, fill], axis=1)
+    kv_heads = key_rot.shape[1] // HEAD_DIM
+    group_size = queries.shape[1] // kv_heads
+    same = jnp.eye(kv_heads, dtype=jnp.bool_)
+    queries = queries.transpose(1, 0, 2).reshape(kv_heads, group_size, tokens, 1, HEAD_DIM)
+    queries = jnp.where(same[:, None, None, :, None], queries, 0).reshape(
+        kv_heads * group_size * tokens, kv_heads * HEAD_DIM
+    )
+    out_rows = w_out.reshape(kv_heads, group_size, 1, HEAD_DIM, width)
+    out_rows = jnp.where(same[:, None, :, None, None], out_rows, 0).reshape(
+        kv_heads * group_size * kv_heads * HEAD_DIM, width
+    )
+    kv = jnp.concatenate([key_rot, value_proj], axis=1)
+    hidden_out = run_layer(
+        queries,
+        kv,
+        table,
+        starts[:, None],
+        hidden,
+        norm_moe[None, :],
+        out_rows,
+        w_gate,
+        w_up,
+        w_down,
+    )
     return hidden_out, kv_cache
 
 

time: 162 us -> 120 us (0.74)
  waiting for transfers between devices: 46.8 us -> 0 us
  Pallas kernels: 72.2 us -> 104 us
  between operations: 14.3 us -> 0.86 us
  matrix products: 13.1 us -> 2.31 us
  other arithmetic: 8.15 us -> 4.64 us
    pallas_call x1, Pallas kernels: 72.2 us -> 104 us  [run_layer(): pl.pallas_call(layer_kernel, out_shape=jax.ShapeDtypeStruct((tokens, widt...]
    all_gather x1 -> x0, waiting for transfers between devices: 27.5 us -> none  [per_device(): lax.all_gather(jnp.concatenate([key_rot, value_proj, high, low], axis=1),...]
    reduce_scatter x1 -> x0, waiting for transfers between devices: 19.3 us -> none  [per_device(): lax.psum_scatter(partial_out.astype(jnp.bfloat16), 'tp', scatter_dimensio...]
    sub x1 -> x0, matrix products: 5.49 us -> none  [attend_all(): weights = jnp.where(allowed, jnp.exp(masked - top), 0.0)]
    dot_general x2 -> x0, matrix products: 4.22 us -> none  [the longest x1 3.1 us: attend_all(): jnp.einsum('kgts,skd->kgtd', weights.astype(jnp.bfloat16), values, prefer...]
    slice x3 -> x0, local copies, waits for them, and re-layouts: 1.69 us -> none  [the longest x2 1.48 us: per_device(): gathered[:, :kv_width]]
  transfers between devices with their start and end apart: 2 -> 0, of which waited for: 2 -> 0; matrix products, arithmetic and copies ran while one was open for 2% -> 0% of each run, Pallas kernels for 0% -> 0%
where the time goes in v3:
time: 120 us; the launch traced here: 118 us
  Pallas kernels  104 us (87%)
  local copies, waits for them, and re-layouts  7.11 us (6%)
  other arithmetic  4.64 us (4%)
  matrix products  2.31 us (2%)
    pallas_call x1, Pallas kernels, run_layer(): pl.pallas_call(layer_kernel, out_shape=jax.ShapeDtypeStruct((tokens, widt...  104 us
    unnamed x16, local copies, waits for them, and re-layouts  4.24 us

profile of v3, /device:TPU:0, one launch (start us, length us, event | category | flops | bytes accessed | tf_op | source)
XLA Modules:
  0.0 118.4 jit_solution(8270674448980333802)
XLA Ops:
  0.6 0.0 copy-start
  0.7 0.1 copy.51
  0.8 0.8 dynamic_slice.3
  1.6 1.0 convert_reduce_fusion
  2.6 0.1 pad.4.clone
  2.7 1.2 %fusion = f32[256]{0:T(256)S(1)} fusion(bf16[256,1024]{1,0:T(8,128)(2,1)} %hidden_ref.1), kind=kLoop, calls=%fused_computation.4 | loop fusion | flops 786176 | bytes 525312 | tf_op jit(solution)/shard_map/reduce_sum | solution.py:20
  4.0 0.1 broadcast_in_dim.94
  4.0 0.1 broadcast_in_dim.95
  4.1 0.7 convert_element_type.46
  4.8 0.7 broadcast_in_dim.93.norm_ref
  5.5 0.0 copy-start.1
  5.5 0.0 copy-start.6
  5.5 0.8 select_reduce_fusion
  6.3 0.1 copy.50
  6.5 0.2 multiply_cosine_fusion
  6.7 1.5 %convolution_convert_fusion = bf16[256,128]{1,0:T(8,128)(2,1)S(1)} fusion(bf16[1024,128]{1,0:T(8,128)(2,1)} %param.21, bf16[256,1024]{1,0:T(8,128)(2,1)} %hidden_ref.1, f32[1024]{0:T(1024)S(1)} %convert_element_type.46, f32[256]{0:T(256)S(1)} %add_rsqrt_fusion), kind=kOutput, calls=%fused_computation.3 | convolution fusion | flops 68190208 | bytes 857088 | tf_op jit(solution)/shard_map/dot_general | solution.py:210
  8.1 0.1 copy.49
  8.2 0.1 maximum_maximum_fusion.table_ref
  8.3 0.0 copy-done.1
  8.4 0.0 copy-done.6
  8.4 0.4 fusion.4
  8.8 0.1 copy.54
  8.9 0.8 copy.55
  9.7 0.1 copy.47
  9.9 0.1 copy.53.starts_ref
  10.0 0.0 copy-done
  10.0 0.4 fusion.6
  10.5 0.0 copy-start.5
  10.6 0.1 copy.45
  10.7 0.3 broadcast_select_fusion
  11.0 0.2 select_n.22
  11.2 0.0 copy-start.2
  11.2 0.2 copy.52.query_ref
  11.3 0.2 copy-done.5
  11.6 0.0 copy-start.3
  11.6 0.1 bitcast_select_fusion.wo_ref
  11.7 0.7 copy-done.2
  12.4 0.5 copy-done.3
  12.9 0.0 copy-start.4
  12.9 1.2 %copy-done.4 = bf16[4,128,1024]{2,1,0:T(8,128)(2,1)S(1)} copy-done((bf16[4,128,1024]{2,1,0:T(8,128)(2,1)S(1)}, bf16[4,128,1024]{2,1,0:T(8,128)(2,1)}, u32[]{:S(2)}) %copy-start.4) | copy-done | bytes 1048600
  14.1 103.5 %layer.1 = bf16[256,1024]{1,0:T(8,128)(2,1)S(1)} custom-call(bf16[1024,128]{1,0:T(8,128)(2,1)S(1)} %copy.52.query_ref, bf16[256,256]{1,0:T(8,128)(2,1)S(1)} %pad_maximum_fusion.1.kv_ref, bf16[256,128]{1,0:T(8,128)(2,1)S(1)} %maximum_maximum_fusion.table_ref, s32[256,1]{1,0:T(8,128)S(1)} %copy.53.starts_ref, bf16[256,1024]{1,0:T(8,128)(2,1)S(1)} %copy-done.1, ...), custom_call_target="tpu_custom_call" | custom-call | flops 6442450944 | bytes 4194304 | tf_op jit(solution)/shard_map/layer/pallas_call | solution.py:570
  117.6 0.8 copy.58
  (13 shorter events, 0.2 us)
Async XLA Ops:
  0.6 9.4 %copy-start = (bf16[1024,256]{1,0:T(8,128)(2,1)S(1)}, bf16[1024,256]{1,0:T(8,128)(2,1)}, u32[]{:S(2)}) copy-start(bf16[1024,256]{1,0:T(8,128)(2,1)} %param.19) | copy-start | bytes 1572868
  5.5 2.9 %copy-start.1 = (bf16[256,1024]{1,0:T(8,128)(2,1)S(1)}, bf16[256,1024]{1,0:T(8,128)(2,1)}, u32[]{:S(2)}) copy-start(bf16[256,1024]{1,0:T(8,128)(2,1)} %hidden_ref.1) | copy-start | bytes 1572868
  5.5 2.9 %copy-start.6 = (bf16[1024,128]{1,0:T(8,128)(2,1)S(1)}, bf16[1024,128]{1,0:T(8,128)(2,1)}, u32[]{:S(2)}) copy-start(bf16[1024,128]{1,0:T(8,128)(2,1)} %param.20) | copy-start | bytes 786436
  10.5 1.0 copy-start.5
  11.2 1.3 %copy-start.2 = (bf16[4,1024,128]{2,1,0:T(8,128)(2,1)S(1)}, bf16[4,1024,128]{2,1,0:T(8,128)(2,1)}, u32[]{:S(2)}) copy-start(bf16[4,1024,128]{2,1,0:T(8,128)(2,1)} %wg_hbm.1) | copy-start | bytes 3145732
  11.6 1.3 %copy-start.3 = (bf16[4,1024,128]{2,1,0:T(8,128)(2,1)S(1)}, bf16[4,1024,128]{2,1,0:T(8,128)(2,1)}, u32[]{:S(2)}) copy-start(bf16[4,1024,128]{2,1,0:T(8,128)(2,1)} %wu_hbm.1) | copy-start | bytes 3145732
  12.9 1.2 %copy-start.4 = (bf16[4,128,1024]{2,1,0:T(8,128)(2,1)S(1)}, bf16[4,128,1024]{2,1,0:T(8,128)(2,1)}, u32[]{:S(2)}) copy-start(bf16[4,128,1024]{2,1,0:T(8,128)(2,1)} %param.25) | copy-start | bytes 3145732

commit v4 on v3

--- a/solution.py
+++ b/solution.py
@@ -239,8 +239,8 @@
 def layer_kernel(
     query_ref, kv_ref, table_ref, starts_ref, hidden_ref, norm_ref, wo_ref,
     wg_hbm, wu_hbm, wd_hbm, out_ref,
-    kv, table, top, norm_sum, mixed, partial_out, from_heads, residual, normed_ref,
-    kv_sem, table_sem, heads_sem,
+    kv, table, top, mixed, wo_all, own_heads, from_heads, residual,
+    kv_sem, table_sem, wo_sem, heads_sem,
     rows, weights, downs, act, parts, from_core, first, second, from_tp,
     weight_sem, send_sem, row_sem, core_sem, first_sem, second_sem, tp_sem, out_sem,
 ):
@@ -299,12 +299,16 @@
             device_id_type=pl.DeviceIdType.MESH,
         ).wait_recv()
 
-    def spread(buffer, sems, parts_of):
+    def spread(buffer, sems, parts_of, place=None):
         def go(mask, k, way):
-            send(buffer.at[mask, k], buffer.at[mask ^ way, k], sems.at[mask ^ way, k], seq_peer[way])
+            if place is None:
+                source, target = buffer.at[mask, k], buffer.at[mask ^ way, k]
+            else:
+                source = target = buffer.at[place(mask, k)]
+            send(source, target, sems.at[mask ^ way, k], seq_peer[way])
 
         def take(mask, k):
-            arrived(buffer.at[mask, k], sems.at[mask, k])
+            arrived(buffer.at[(mask, k) if place is None else place(mask, k)], sems.at[mask, k])
 
         def sides(k):
             take(XDIR, k)
@@ -328,6 +332,20 @@
     for k in halves:
         for way in (XDIR, YDIR, CORE):
             kv_go(0, k, way)
+
+    share = wo_ref.shape[0] // kv.shape[0]
+
+    def wo_place(mask, k):
+        start = ((tp + k) % n_tp) * wo_ref.shape[0] + flip(me, mask) * share
+        return pl.ds(pl.multiple_of(start, share), share)
+
+    wo_go, wo_take, wo_sides = spread(wo_all, wo_sem, n_tp, wo_place)
+    wo_own = wo_all.at[wo_place(0, 0)]
+    wo_own[...] = wo_ref[pl.ds(pl.multiple_of(me * share, share), share), :]
+    for k in (2, 1, 3):
+        send(wo_own, wo_own, wo_sem.at[0, n_tp - k], tp_peer[k])
+    for way in (XDIR, YDIR, CORE):
+        wo_go(0, 0, way)
     for k in halves:
         for way in (XDIR, YDIR, CORE):
             table_go(0, k, way)
@@ -335,96 +353,117 @@
     tokens = 2 * half
     kv_width = kv.shape[3] // 2
     heads = query_ref.shape[0] // tokens
-    top[...] = jnp.full(top.shape, -1e30, jnp.float32)
-    norm_sum[...] = jnp.zeros(norm_sum.shape, jnp.float32)
+    top[...] = jnp.full(top.shape, -3e38, jnp.float32)
     mixed[...] = jnp.zeros(mixed.shape, jnp.float32)
 
-    def attend(mask):
-        block_kv = kv[mask].reshape(tokens, 2 * kv_width)
-        keys, values = block_kv[:, :kv_width], block_kv[:, kv_width:]
+    def attend(masks):
+        count = len(masks) * tokens
+        blocks = [kv[mask].reshape(tokens, 2 * kv_width) for mask in masks]
+        keys = jnp.concatenate([one[:, :kv_width] for one in blocks], axis=0)
+        values = jnp.concatenate([one[:, kv_width:] for one in blocks], axis=0)
+        values = jnp.concatenate([values, jnp.ones_like(values)], axis=1)
         query_index = me * tokens + lax.broadcasted_iota(jnp.int32, (tokens, tokens), 0)
-        key_index = flip(me, mask) * tokens + lax.broadcasted_iota(
-            jnp.int32, (tokens, tokens), 1
-        )
-        allowed = (key_index <= query_index) & (key_index >= starts_ref[...])
+        local = lax.broadcasted_iota(jnp.int32, (tokens, tokens), 1)
+        allowed = []
+        for mask in masks:
+            key_index = flip(me, mask) * tokens + local
+            allowed.append((key_index <= query_index) & (key_index >= starts_ref[...]))
 
         for head in range(heads):
             span = pl.ds(head * tokens, tokens)
-            scores = (
-                lax.dot_general(
-                    query_ref[span, :],
-                    keys,
-                    (((1,), (1,)), ((), ())),
-                    preferred_element_type=jnp.float32,
-                )
-                * SCORE_SCALE
+            scores = lax.dot_general(
+                query_ref[span, :],
+                keys,
+                (((1,), (1,)), ((), ())),
+                preferred_element_type=jnp.float32,
             )
-            masked = jnp.where(allowed, scores, -1e30)
+            masked = [
+                jnp.where(ok, scores[:, n * tokens : (n + 1) * tokens], -3e38)
+                for n, ok in enumerate(allowed)
+            ]
+            highest = masked[0]
+            for one in masked[1:]:
+                highest = jnp.maximum(highest, one)
             old_top = top[span, :]
-            new_top = jnp.maximum(old_top, jnp.max(masked, axis=1, keepdims=True))
-            weights_now = jnp.where(allowed, jnp.exp(masked - new_top), 0.0)
+            new_top = jnp.maximum(old_top, jnp.max(highest, axis=1, keepdims=True))
             factor = jnp.exp(old_top - new_top)
             top[span, :] = new_top
-            norm_sum[span, :] = norm_sum[span, :] * factor + jnp.sum(
-                weights_now, axis=1, keepdims=True
+            weights_now = jnp.concatenate(
+                [jnp.exp(one - new_top).astype(jnp.bfloat16) for one in masked], axis=1
             )
             mixed[span, :] = mixed[span, :] * factor + jnp.dot(
-                weights_now.astype(jnp.bfloat16), values, preferred_element_type=jnp.float32
+                weights_now, values, preferred_element_type=jnp.float32
             )
 
-    attend(0)
+    diagonal = XDIR + YDIR
+    attend((0,))
     for k in halves:
         kv_sides(k)
+    for k in (1, 3, 2):
+        wo_take(0, k)
+        for way in (XDIR, YDIR, CORE):
+            wo_go(0, k, way)
     for k in halves:
         kv_take(CORE, k)
-    attend(XDIR)
-    attend(YDIR)
-    for k in halves:
-        kv_take(XDIR + YDIR, k)
-        kv_go(XDIR + YDIR, k, CORE)
-    attend(CORE)
+    attend((CORE, XDIR, YDIR))
+    for k in halves:
+        kv_take(diagonal, k)
+        kv_go(diagonal, k, CORE)
+    for k in range(n_tp):
+        wo_sides(k)
     for k in halves:
         table_sides(k)
-    attend(XDIR + YDIR)
-    for mask in (XDIR + CORE, YDIR + CORE, XDIR + YDIR + CORE):
+    for mask in (XDIR + CORE, YDIR + CORE):
         for k in halves:
             kv_take(mask, k)
-        attend(mask)
-    for k in halves:
-        table_take(XDIR + YDIR, k)
-        table_go(XDIR + YDIR, k, CORE)
-
-    attended = jnp.concatenate(
-        [
-            (mixed[pl.ds(h * tokens, tokens), :] / norm_sum[pl.ds(h * tokens, tokens), :]).astype(
-                jnp.bfloat16
-            )
-            for h in range(heads)
-        ],
-        axis=1,
-    )
-    step = 256
-    for column in range(0, width, step):
-        partial_out[:, column : column + step] = jnp.dot(
-            attended, wo_ref[:, column : column + step], preferred_element_type=jnp.float32
-        ).astype(jnp.bfloat16)
+    attend((XDIR + CORE, YDIR + CORE))
+    for k in range(n_tp):
+        wo_take(diagonal, k)
+        wo_go(diagonal, k, CORE)
+    for k in halves:
+        table_take(diagonal, k)
+        table_go(diagonal, k, CORE)
+    for k in halves:
+        kv_take(diagonal + CORE, k)
+    attend((diagonal, diagonal + CORE))
+
+    lane_head = lax.broadcasted_iota(jnp.int32, (tokens, kv_width), 1) // HEAD_DIM
+    kv_heads = kv_width // HEAD_DIM
+    group_size = heads // kv_heads
+    for g in range(group_size):
+        joined = jnp.zeros((tokens, kv_width), jnp.float32)
+        for j in range(kv_heads):
+            span = pl.ds((j * group_size + g) * tokens, tokens)
+            ratio = mixed[span, :kv_width] / mixed[span, kv_width:]
+            joined = jnp.where(lane_head == j, ratio, joined)
+        own_heads[:, g * kv_width : (g + 1) * kv_width] = joined.astype(jnp.bfloat16)
 
     def block_rows(k):
         return pl.ds(pl.multiple_of(((tp + k) % n_tp) * block, block), block)
 
     for k in (2, 1, 3):
         back = n_tp - k
-        send(partial_out.at[block_rows(k)], from_heads.at[back], heads_sem.at[back], tp_peer[k])
-    summed = partial_out[block_rows(0), :].astype(jnp.float32)
+        send(own_heads.at[block_rows(k)], from_heads.at[back], heads_sem.at[back], tp_peer[k])
+    for mask in (CORE, XDIR + CORE, YDIR + CORE, diagonal + CORE):
+        for k in range(n_tp):
+            wo_take(mask, k)
+
+    def project(block_heads, k):
+        depth = wo_ref.shape[0]
+        start = pl.multiple_of(((tp + k) % n_tp) * depth, depth)
+        return jnp.dot(
+            block_heads, wo_all[pl.ds(start, depth), :], preferred_element_type=jnp.float32
+        )
+
+    summed = project(own_heads[block_rows(0), :], 0)
     for k in (1, 3, 2):
         arrived(from_heads.at[k], heads_sem.at[k])
-        summed = summed + from_heads[k].astype(jnp.float32)
+        summed = summed + project(from_heads[k], k)
     added = hidden_ref[block_rows(0), :].astype(jnp.float32) + summed
     residual[...] = added.astype(jnp.bfloat16)
-    normed_ref[...] = normalize_rows(residual[...], norm_ref[...]).astype(jnp.bfloat16)
 
     pass_on, take, handle_sides = spread(rows, row_sem, n_tp)
-    rows[0, 0] = normed_ref[...]
+    rows[0, 0] = normalize_rows(residual[...], norm_ref[...]).astype(jnp.bfloat16)
     for k in (2, 1, 3):
         back = n_tp - k
         send(rows.at[0, 0], rows.at[0, back], row_sem.at[0, back], tp_peer[k])
@@ -459,6 +498,7 @@
             act[:, n * units : (n + 1) * units] = jnp.where(scale > 0, value, 0.0).astype(
                 jnp.bfloat16
             )
+        step = 256
         for column in range(0, width, step):
             piece = jnp.dot(
                 act[...],
@@ -497,23 +537,20 @@
     compute(1)
     give_core(1)
     compute(2)
+    compute(4)
+    for mask in (XDIR + CORE, YDIR + CORE):
+        for k in range(n_tp):
+            take(mask, k)
+        compute(mask)
+        give_core(mask)
     for k in range(n_tp):
-        take(XDIR + CORE, k)
-    compute(3)
-    give_core(3)
+        take(diagonal, k)
+        pass_on(diagonal, k, CORE)
+    compute(diagonal)
     for k in range(n_tp):
-        take(YDIR + XDIR, k)
-        pass_on(YDIR + XDIR, k, CORE)
-    for k in range(n_tp):
-        take(YDIR + CORE, k)
-    compute(5)
-    give_core(5)
-    compute(4)
-    for k in range(n_tp):
-        take(YDIR + XDIR + CORE, k)
-    compute(7)
-    give_core(7)
-    compute(6)
+        take(diagonal + CORE, k)
+    compute(diagonal + CORE)
+    give_core(diagonal + CORE)
 
     early = ((XDIR, YDIR, (1, 0)), (YDIR, XDIR, (2, 3)))
 
@@ -529,11 +566,10 @@
     for way, other, ks in early:
         give_first(XDIR + YDIR, way, ks)
     add_core(0)
-    for way, other, ks in early:
-        for k in ks:
-            arrived(first.at[1, k], first_sem.at[1, k])
-            add(other, k, first[1, k])
-            send(parts.at[other, k], second.at[k], second_sem.at[k], seq_peer[other])
+    for other, k in ((YDIR, 1), (XDIR, 2), (YDIR, 0), (XDIR, 3)):
+        arrived(first.at[1, k], first_sem.at[1, k])
+        add(other, k, first[1, k])
+        send(parts.at[other, k], second.at[k], second_sem.at[k], seq_peer[other])
     for k in (2, 1, 3, 0):
         arrived(first.at[0, k], first_sem.at[0, k])
         add(0, k, first[0, k])
@@ -577,14 +613,14 @@
             pltpu.VMEM((n_seq, 2, tokens // 2, kv.shape[1]), bf16),
             pltpu.VMEM((n_seq, 2, tokens // 2, table.shape[1]), bf16),
             pltpu.VMEM((queries.shape[0], 1), f32),
-            pltpu.VMEM((queries.shape[0], 1), f32),
-            pltpu.VMEM((queries.shape[0], lanes), f32),
-            pltpu.VMEM((tokens, width), bf16),
-            pltpu.VMEM((n_tp, block, width), bf16),
-            pltpu.VMEM((block, width), bf16),
+            pltpu.VMEM((queries.shape[0], 2 * lanes), f32),
+            pltpu.VMEM((n_tp * w_out.shape[0], width), bf16),
+            pltpu.VMEM((tokens, w_out.shape[0]), bf16),
+            pltpu.VMEM((n_tp, block, w_out.shape[0]), bf16),
             pltpu.VMEM((block, width), bf16),
             pltpu.SemaphoreType.DMA((n_seq, 2)),
             pltpu.SemaphoreType.DMA((n_seq, 2)),
+            pltpu.SemaphoreType.DMA((n_seq, n_tp)),
             pltpu.SemaphoreType.DMA((n_tp,)),
             pltpu.VMEM((n_seq, n_tp, block, width), bf16),
             pltpu.VMEM((slots, width, 2 * units), bf16),
@@ -596,7 +632,7 @@
             pltpu.VMEM((n_tp, block, width), bf16),
             pltpu.VMEM((n_tp, block, width), bf16),
             pltpu.SemaphoreType.DMA((2 * slots + 1,)),
-            pltpu.SemaphoreType.DMA((112,)),
+            pltpu.SemaphoreType.DMA((144,)),
             pltpu.SemaphoreType.DMA((n_seq, n_tp)),
             pltpu.SemaphoreType.DMA((n_seq // 2,)),
             pltpu.SemaphoreType.DMA((2, n_tp)),
@@ -653,13 +689,11 @@
     group_size = queries.shape[1] // kv_heads
     same = jnp.eye(kv_heads, dtype=jnp.bool_)
     queries = queries.transpose(1, 0, 2).reshape(kv_heads, group_size, tokens, 1, HEAD_DIM)
-    queries = jnp.where(same[:, None, None, :, None], queries, 0).reshape(
+    queries = jnp.where(same[:, None, None, :, None], queries * SCORE_SCALE, 0).reshape(
         kv_heads * group_size * tokens, kv_heads * HEAD_DIM
     )
-    out_rows = w_out.reshape(kv_heads, group_size, 1, HEAD_DIM, width)
-    out_rows = jnp.where(same[:, None, :, None, None], out_rows, 0).reshape(
-        kv_heads * group_size * kv_heads * HEAD_DIM, width
-    )
+    out_rows = w_out.reshape(kv_heads, group_size, HEAD_DIM, width).transpose(1, 0, 2, 3)
+    out_rows = out_rows.reshape(w_out.shape)
     kv = jnp.concatenate([key_rot, value_proj], axis=1)
     hidden_out = run_layer(
         queries,

time: 120 us -> 114 us (0.950)
  Pallas kernels: 104 us -> 98.9 us
    pallas_call x1, Pallas kernels: 104 us -> 98.9 us  [run_layer(): pl.pallas_call(layer_kernel, out_shape=jax.ShapeDtypeStruct((tokens, widt...]
where the time goes in v4:
time: 114 us
  Pallas kernels  98.9 us (87%)
  local copies, waits for them, and re-layouts  6.99 us (6%)
  other arithmetic  4.52 us (4%)
  matrix products  2.3 us (2%)
    pallas_call x1, Pallas kernels, run_layer(): pl.pallas_call(layer_kernel, out_shape=jax.ShapeDtypeStruct((tokens, widt...  98.9 us
    unnamed x16, local copies, waits for them, and re-layouts  4.33 us

profile of v4, /device:TPU:0, one launch (start us, length us, event | category | flops | bytes accessed | tf_op | source)
XLA Modules:
  0.0 113.6 jit_solution(10790979909899015302)
XLA Ops:
  0.6 0.0 copy-start
  0.6 0.8 dynamic_slice.3
  1.5 1.0 convert_reduce_fusion
  2.5 0.1 pad.4.clone
  2.6 1.2 %fusion = f32[256]{0:T(256)S(1)} fusion(bf16[256,1024]{1,0:T(8,128)(2,1)} %hidden_ref.1), kind=kLoop, calls=%fused_computation.4 | loop fusion | flops 786176 | bytes 525312 | tf_op jit(solution)/shard_map/reduce_sum | solution.py:20
  3.9 0.7 convert_element_type.44
  4.6 0.7 broadcast_in_dim.61.norm_ref
  5.2 0.0 copy-start.1
  5.2 0.0 copy-start.6
  5.2 0.8 select_reduce_fusion
  6.1 0.1 copy.51
  6.2 0.2 multiply_cosine_fusion
  6.4 1.5 %convolution_convert_fusion = bf16[256,128]{1,0:T(8,128)(2,1)S(1)} fusion(bf16[1024,128]{1,0:T(8,128)(2,1)} %param.21, bf16[256,1024]{1,0:T(8,128)(2,1)} %hidden_ref.1, f32[1024]{0:T(1024)S(1)} %convert_element_type.44, f32[256]{0:T(256)S(1)} %add_rsqrt_fusion), kind=kOutput, calls=%fused_computation.3 | convolution fusion | flops 68190208 | bytes 857088 | tf_op jit(solution)/shard_map/dot_general | solution.py:210
  7.9 0.1 copy.50
  8.0 0.1 maximum_maximum_fusion.table_ref
  8.1 0.0 copy-done.1
  8.1 0.0 copy-done.6
  8.1 0.4 fusion.4
  8.5 0.1 copy.55
  8.7 0.8 copy.56
  9.5 0.1 copy.48
  9.6 0.1 copy.54.starts_ref
  9.8 0.0 copy-done
  9.8 0.4 fusion.6
  10.3 0.0 copy-start.5
  10.3 0.1 copy.46
  10.5 0.3 broadcast_select_fusion
  10.7 0.0 copy-start.2
  10.7 0.2 select_n.17
  10.9 0.2 copy.53.query_ref
  11.1 0.2 copy-done.5
  11.3 0.0 copy-start.3
  11.4 0.6 copy-done.2
  12.0 0.6 copy-done.3
  12.6 0.0 copy-start.4
  12.6 1.2 %copy-done.4 = bf16[4,128,1024]{2,1,0:T(8,128)(2,1)S(1)} copy-done((bf16[4,128,1024]{2,1,0:T(8,128)(2,1)S(1)}, bf16[4,128,1024]{2,1,0:T(8,128)(2,1)}, u32[]{:S(2)}) %copy-start.4) | copy-done | bytes 1048600
  13.9 98.9 %layer.1 = bf16[256,1024]{1,0:T(8,128)(2,1)S(1)} custom-call(bf16[1024,128]{1,0:T(8,128)(2,1)S(1)} %copy.53.query_ref, bf16[256,256]{1,0:T(8,128)(2,1)S(1)} %pad_maximum_fusion.kv_ref, bf16[256,128]{1,0:T(8,128)(2,1)S(1)} %maximum_maximum_fusion.table_ref, s32[256,1]{1,0:T(8,128)S(1)} %copy.54.starts_ref, bf16[256,1024]{1,0:T(8,128)(2,1)S(1)} %copy-done.1, ...), custom_call_target="tpu_custom_call" | custom-call | flops 6442450944 | bytes 4194304 | tf_op jit(solution)/shard_map/layer/pallas_call | solution.py:606
  112.8 0.8 copy.59
  (14 shorter events, 0.2 us)
Async XLA Ops:
  0.6 9.1 %copy-start = (bf16[1024,256]{1,0:T(8,128)(2,1)S(1)}, bf16[1024,256]{1,0:T(8,128)(2,1)}, u32[]{:S(2)}) copy-start(bf16[1024,256]{1,0:T(8,128)(2,1)} %param.19) | copy-start | bytes 1572868
  5.2 2.9 %copy-start.1 = (bf16[256,1024]{1,0:T(8,128)(2,1)S(1)}, bf16[256,1024]{1,0:T(8,128)(2,1)}, u32[]{:S(2)}) copy-start(bf16[256,1024]{1,0:T(8,128)(2,1)} %hidden_ref.1) | copy-start | bytes 1572868
  5.2 2.9 %copy-start.6 = (bf16[1024,128]{1,0:T(8,128)(2,1)S(1)}, bf16[1024,128]{1,0:T(8,128)(2,1)}, u32[]{:S(2)}) copy-start(bf16[1024,128]{1,0:T(8,128)(2,1)} %param.20) | copy-start | bytes 786436
  10.3 1.0 copy-start.5
  10.7 1.3 %copy-start.2 = (bf16[4,1024,128]{2,1,0:T(8,128)(2,1)S(1)}, bf16[4,1024,128]{2,1,0:T(8,128)(2,1)}, u32[]{:S(2)}) copy-start(bf16[4,1024,128]{2,1,0:T(8,128)(2,1)} %wg_hbm.1) | copy-start | bytes 3145732
  11.3 1.3 %copy-start.3 = (bf16[4,1024,128]{2,1,0:T(8,128)(2,1)S(1)}, bf16[4,1024,128]{2,1,0:T(8,128)(2,1)}, u32[]{:S(2)}) copy-start(bf16[4,1024,128]{2,1,0:T(8,128)(2,1)} %wu_hbm.1) | copy-start | bytes 3145732
  12.6 1.2 %copy-start.4 = (bf16[4,128,1024]{2,1,0:T(8,128)(2,1)S(1)}, bf16[4,128,1024]{2,1,0:T(8,128)(2,1)}, u32[]{:S(2)}) copy-start(bf16[4,128,1024]{2,1,0:T(8,128)(2,1)} %param.25) | copy-start | bytes 3145732

commit v5 on v4

--- a/solution.py
+++ b/solution.py
@@ -239,7 +239,7 @@
 def layer_kernel(
     query_ref, kv_ref, table_ref, starts_ref, hidden_ref, norm_ref, wo_ref,
     wg_hbm, wu_hbm, wd_hbm, out_ref,
-    kv, table, top, mixed, wo_all, own_heads, from_heads, residual,
+    kv, table, hidden_rows, top, mixed, wo_all, own_heads, from_heads, residual,
     kv_sem, table_sem, wo_sem, heads_sem,
     rows, weights, downs, act, parts, from_core, first, second, from_tp,
     weight_sem, send_sem, row_sem, core_sem, first_sem, second_sem, tp_sem, out_sem,
@@ -264,6 +264,21 @@
                 )
             )
     loads.append(pltpu.make_async_copy(wd_hbm, downs, weight_sem.at[2 * slots]))
+    share = wo_ref.shape[0] // kv.shape[0]
+    own_share = pltpu.make_async_copy(
+        wo_ref.at[pl.ds(pl.multiple_of(me * share, share), share)],
+        wo_all.at[
+            pl.ds(pl.multiple_of(tp * wo_ref.shape[0] + me * share, share), share)
+        ],
+        weight_sem.at[2 * slots + 1],
+    )
+    own_share.start()
+    own_hidden = pltpu.make_async_copy(
+        hidden_ref.at[pl.ds(pl.multiple_of(tp * block, block), block)],
+        hidden_rows,
+        weight_sem.at[2 * slots + 2],
+    )
+    own_hidden.start()
     for load in loads:
         load.start()
 
@@ -333,15 +348,13 @@
         for way in (XDIR, YDIR, CORE):
             kv_go(0, k, way)
 
-    share = wo_ref.shape[0] // kv.shape[0]
-
     def wo_place(mask, k):
         start = ((tp + k) % n_tp) * wo_ref.shape[0] + flip(me, mask) * share
         return pl.ds(pl.multiple_of(start, share), share)
 
     wo_go, wo_take, wo_sides = spread(wo_all, wo_sem, n_tp, wo_place)
     wo_own = wo_all.at[wo_place(0, 0)]
-    wo_own[...] = wo_ref[pl.ds(pl.multiple_of(me * share, share), share), :]
+    own_share.wait()
     for k in (2, 1, 3):
         send(wo_own, wo_own, wo_sem.at[0, n_tp - k], tp_peer[k])
     for way in (XDIR, YDIR, CORE):
@@ -459,7 +472,8 @@
     for k in (1, 3, 2):
         arrived(from_heads.at[k], heads_sem.at[k])
         summed = summed + project(from_heads[k], k)
-    added = hidden_ref[block_rows(0), :].astype(jnp.float32) + summed
+    own_hidden.wait()
+    added = hidden_rows[...].astype(jnp.float32) + summed
     residual[...] = added.astype(jnp.bfloat16)
 
     pass_on, take, handle_sides = spread(rows, row_sem, n_tp)
@@ -606,12 +620,14 @@
     return pl.pallas_call(
         layer_kernel,
         out_shape=jax.ShapeDtypeStruct((tokens, width), bf16),
-        in_specs=[pl.BlockSpec(memory_space=pltpu.VMEM)] * 7
-        + [pl.BlockSpec(memory_space=pl.ANY)] * 3,
+        in_specs=[pl.BlockSpec(memory_space=pltpu.VMEM)] * 4
+        + [pl.BlockSpec(memory_space=pl.ANY), pl.BlockSpec(memory_space=pltpu.VMEM)]
+        + [pl.BlockSpec(memory_space=pl.ANY)] * 4,
         out_specs=pl.BlockSpec(memory_space=pltpu.VMEM),
         scratch_shapes=[
             pltpu.VMEM((n_seq, 2, tokens // 2, kv.shape[1]), bf16),
             pltpu.VMEM((n_seq, 2, tokens // 2, table.shape[1]), bf16),
+            pltpu.VMEM((block, width), bf16),
             pltpu.VMEM((queries.shape[0], 1), f32),
             pltpu.VMEM((queries.shape[0], 2 * lanes), f32),
             pltpu.VMEM((n_tp * w_out.shape[0], width), bf16),
@@ -631,7 +647,7 @@
             pltpu.VMEM((2, n_tp, block, width), bf16),
             pltpu.VMEM((n_tp, block, width), bf16),
             pltpu.VMEM((n_tp, block, width), bf16),
-            pltpu.SemaphoreType.DMA((2 * slots + 1,)),
+            pltpu.SemaphoreType.DMA((2 * slots + 3,)),
             pltpu.SemaphoreType.DMA((144,)),
             pltpu.SemaphoreType.DMA((n_seq, n_tp)),
             pltpu.SemaphoreType.DMA((n_seq // 2,)),

time: 114 us -> 114 us (level)
  no operation moved by 1% of the time
where the time goes in v5:
time: 114 us
  Pallas kernels  99.2 us (87%)
  local copies, waits for them, and re-layouts  6.99 us (6%)
  other arithmetic  4.52 us (4%)
  matrix products  2.3 us (2%)
    pallas_call x1, Pallas kernels, run_layer(): pl.pallas_call(layer_kernel, out_shape=jax.ShapeDtypeStruct((tokens, widt...  99.2 us
    unnamed x16, local copies, waits for them, and re-layouts  4.33 us

profile of v5, /device:TPU:0, one launch (start us, length us, event | category | flops | bytes accessed | tf_op | source)
XLA Modules:
  0.0 113.9 jit_solution(14961662419702938496)
XLA Ops:
  0.6 0.0 copy-start
  0.6 0.8 dynamic_slice.3
  1.5 1.0 convert_reduce_fusion
  2.5 0.1 pad.4.clone
  2.6 1.2 %fusion = f32[256]{0:T(256)S(1)} fusion(bf16[256,1024]{1,0:T(8,128)(2,1)} %hidden_ref.1), kind=kLoop, calls=%fused_computation.4 | loop fusion | flops 786176 | bytes 525312 | tf_op jit(solution)/shard_map/reduce_sum | solution.py:20
  3.9 0.7 convert_element_type.44
  4.6 0.7 broadcast_in_dim.61.norm_ref
  5.2 0.0 copy-start.1
  5.2 0.0 copy-start.6
  5.2 0.8 select_reduce_fusion
  6.1 0.1 copy.51
  6.2 0.2 multiply_cosine_fusion
  6.4 1.5 %convolution_convert_fusion = bf16[256,128]{1,0:T(8,128)(2,1)S(1)} fusion(bf16[1024,128]{1,0:T(8,128)(2,1)} %param.21, bf16[256,1024]{1,0:T(8,128)(2,1)} %hidden_ref.1, f32[1024]{0:T(1024)S(1)} %convert_element_type.44, f32[256]{0:T(256)S(1)} %add_rsqrt_fusion), kind=kOutput, calls=%fused_computation.3 | convolution fusion | flops 68190208 | bytes 857088 | tf_op jit(solution)/shard_map/dot_general | solution.py:210
  7.9 0.1 copy.50
  8.0 0.1 maximum_maximum_fusion.table_ref
  8.1 0.0 copy-done.1
  8.1 0.0 copy-done.6
  8.1 0.4 fusion.4
  8.5 0.1 copy.55
  8.7 0.8 copy.56
  9.5 0.1 copy.48
  9.6 0.1 copy.54.starts_ref
  9.8 0.0 copy-done
  9.8 0.4 fusion.6
  10.3 0.0 copy-start.5
  10.3 0.1 copy.46
  10.5 0.3 broadcast_select_fusion
  10.7 0.0 copy-start.2
  10.7 0.2 select_n.17
  10.9 0.2 copy.53.query_ref
  11.1 0.2 copy-done.5
  11.3 0.0 copy-start.3
  11.4 0.6 copy-done.2
  12.0 0.6 copy-done.3
  12.6 0.0 copy-start.4
  12.6 1.2 %copy-done.4 = bf16[4,128,1024]{2,1,0:T(8,128)(2,1)S(1)} copy-done((bf16[4,128,1024]{2,1,0:T(8,128)(2,1)S(1)}, bf16[4,128,1024]{2,1,0:T(8,128)(2,1)}, u32[]{:S(2)}) %copy-start.4) | copy-done | bytes 1048600
  13.9 99.2 %layer.1 = bf16[256,1024]{1,0:T(8,128)(2,1)S(1)} custom-call(bf16[1024,128]{1,0:T(8,128)(2,1)S(1)} %copy.53.query_ref, bf16[256,256]{1,0:T(8,128)(2,1)S(1)} %pad_maximum_fusion.kv_ref, bf16[256,128]{1,0:T(8,128)(2,1)S(1)} %maximum_maximum_fusion.table_ref, s32[256,1]{1,0:T(8,128)S(1)} %copy.54.starts_ref, bf16[256,1024]{1,0:T(8,128)(2,1)S(1)} %copy-done.1, ...), custom_call_target="tpu_custom_call" | custom-call | flops 6442450944 | bytes 4194304 | tf_op jit(solution)/shard_map/layer/pallas_call | solution.py:620
  113.1 0.8 copy.59
  (14 shorter events, 0.2 us)
Async XLA Ops:
  0.6 9.1 %copy-start = (bf16[1024,256]{1,0:T(8,128)(2,1)S(1)}, bf16[1024,256]{1,0:T(8,128)(2,1)}, u32[]{:S(2)}) copy-start(bf16[1024,256]{1,0:T(8,128)(2,1)} %param.19) | copy-start | bytes 1572868
  5.2 2.9 %copy-start.1 = (bf16[256,1024]{1,0:T(8,128)(2,1)S(1)}, bf16[256,1024]{1,0:T(8,128)(2,1)}, u32[]{:S(2)}) copy-start(bf16[256,1024]{1,0:T(8,128)(2,1)} %hidden_ref.1) | copy-start | bytes 1572868
  5.2 2.9 %copy-start.6 = (bf16[1024,128]{1,0:T(8,128)(2,1)S(1)}, bf16[1024,128]{1,0:T(8,128)(2,1)}, u32[]{:S(2)}) copy-start(bf16[1024,128]{1,0:T(8,128)(2,1)} %param.20) | copy-start | bytes 786436
  10.3 1.0 copy-start.5
  10.7 1.3 %copy-start.2 = (bf16[4,1024,128]{2,1,0:T(8,128)(2,1)S(1)}, bf16[4,1024,128]{2,1,0:T(8,128)(2,1)}, u32[]{:S(2)}) copy-start(bf16[4,1024,128]{2,1,0:T(8,128)(2,1)} %wg_hbm.1) | copy-start | bytes 3145732
  11.3 1.3 %copy-start.3 = (bf16[4,1024,128]{2,1,0:T(8,128)(2,1)S(1)}, bf16[4,1024,128]{2,1,0:T(8,128)(2,1)}, u32[]{:S(2)}) copy-start(bf16[4,1024,128]{2,1,0:T(8,128)(2,1)} %wu_hbm.1) | copy-start | bytes 3145732
  12.6 1.2 %copy-start.4 = (bf16[4,128,1024]{2,1,0:T(8,128)(2,1)S(1)}, bf16[4,128,1024]{2,1,0:T(8,128)(2,1)}, u32[]{:S(2)}) copy-start(bf16[4,128,1024]{2,1,0:T(8,128)(2,1)} %param.25) | copy-start | bytes 3145732
